TPU v7x, 32 devices: a whole 2x2x4 slice. The times are simulated.
32 devices in a mesh: pts: 8 (over y, x, core), fn: 4 (over z).
Axes of the slice: x: 2, y: 2, z: 4, core: 2. Of those that a mesh axis runs over, the one named last changes fastest.
Arguments:
- query_feats: float32 [32768, 128], P(('pts', 'fn')), may hold values from -6 to 6
- query_coords: float32 [3, 32768], P(None, ('pts', 'fn')), may hold values from 0 to 1
- func_feats: float32 [3, 2048, 128], P(None, 'fn'), may hold values from -6 to 6
- func_counts: int32 [3], replicated, may hold values from 1 to 2048, as said below
- func_present: int32 [3], replicated, may hold values from 0 to 1, as said below
- attn_proj: float32 [2, 2, 3, 128, 128], replicated, may hold values from -1 to 1
- attn_out: float32 [2, 2, 128, 128], replicated, may hold values from -1 to 1
- norm_gain: float32 [2, 5, 128], replicated, may hold values from 0.5 to 1.5
- norm_bias: float32 [2, 5, 128], replicated, may hold values from -3 to 3
- exp_w_in: float32 [2, 2, 4, 128, 256], replicated, may hold values from -0.5 to 0.5
- exp_b_in: float32 [2, 2, 4, 256], replicated, may hold values from -1.5 to 1.5
- exp_w_out: float32 [2, 2, 4, 256, 128], replicated, may hold values from -0.75 to 0.75
- exp_b_out: float32 [2, 2, 4, 128], replicated, may hold values from -1.5 to 1.5
- gate_w_in: float32 [2, 2, 3, 128], replicated, may hold values from -6 to 6
- gate_b_in: float32 [2, 2, 128], replicated, may hold values from -6 to 6
- gate_w_out: float32 [2, 2, 4, 128], replicated, may hold values from -1 to 1
- out_cot: float32 [32768, 128], P(('pts', 'fn')), may hold values from -6 to 6
Outputs:
- query_out: float32 [32768, 128], P(('pts', 'fn'))
- query_grad: float32 [32768, 128], P(('pts', 'fn'))
- func_grad: float32 [3, 2048, 128], P(None, 'fn')
- grad_attn_proj: float32 [2, 2, 3, 128, 128], replicated
- grad_attn_out: float32 [2, 2, 128, 128], replicated
- grad_norm_gain: float32 [2, 5, 128], replicated
- grad_norm_bias: float32 [2, 5, 128], replicated
- grad_exp_w_in: float32 [2, 2, 4, 128, 256], replicated
- grad_exp_b_in: float32 [2, 2, 4, 256], replicated
- grad_exp_w_out: float32 [2, 2, 4, 256, 128], replicated
- grad_exp_b_out: float32 [2, 2, 4, 128], replicated
- grad_gate_w_in: float32 [2, 2, 3, 128], replicated
- grad_gate_b_in: float32 [2, 2, 128], replicated
- grad_gate_w_out: float32 [2, 2, 4, 128], replicated
Inputs may be any that keep to these rules, and one draw needn't show every extreme that they name: `func_counts`: one function, drawn from the seed, has exactly 2048 valid points; a function's valid points are its first ones. `func_present`: the function with 2048 valid points is always present.
All inputs are finite; a program needn't handle non-finite values.
Results may differ from a plain program's by a relative error of at most 0.0003.
Values sent between devices are 32-bit elements; how exact they have to be, the bound alone decides.
A program may use at most 192 MiB of HBM per device.

v0:
```python
import jax
import jax.numpy as jnp
from jax import lax
from jax.sharding import PartitionSpec as P

HEADS = 8
HEAD_SIZE = 16
LAYERS = 2


precise = lax.Precision.HIGHEST


def layer_norm(stream, gain_vec, bias_vec):
    average = jnp.mean(stream, axis=-1, keepdims=True)
    centred = stream - average
    variance = jnp.mean(centred * centred, axis=-1, keepdims=True)
    return centred * lax.rsqrt(variance + 1e-05) * gain_vec + bias_vec


def head_softmax(values):
    shaped = values.reshape(values.shape[:-1] + (HEADS, HEAD_SIZE))
    return jax.nn.softmax(shaped, axis=-1)


def function_summary(func_rows, row_mask, key_weight, value_weight, gain_vec, bias_vec):
    normed = layer_norm(func_rows, gain_vec, bias_vec)
    key_soft = head_softmax(jnp.einsum("frd,de->fre", normed, key_weight, precision=precise))
    values = jnp.einsum("frd,de->fre", normed, value_weight, precision=precise).reshape(
        key_soft.shape
    )
    weighted = key_soft * row_mask[:, :, None, None]
    summary = jnp.einsum("frha,frhb->fhab", weighted, values, precision=precise)
    return (summary, jnp.sum(weighted, axis=1))


def cross_block(stream, query_weight, out_weight, gain_vec, bias_vec, summary, totals, func_share):
    normed = layer_norm(stream, gain_vec, bias_vec)
    queries = head_softmax(jnp.dot(normed, query_weight, precision=precise))
    numerator = jnp.einsum("rha,fhab->frhb", queries, summary, precision=precise)
    denominator = jnp.einsum("rha,fha->frh", queries, totals, precision=precise)
    blended = jnp.einsum(
        "frhb,f->rhb", numerator / denominator[..., None], func_share, precision=precise
    )
    return stream + jnp.dot(blended.reshape(stream.shape), out_weight, precision=precise)


def expert_block(
    stream, coords, gain_vec, bias_vec, w_in, b_in, w_out, b_out, gate_in, gate_bias, gate_out
):
    normed = layer_norm(stream, gain_vec, bias_vec)
    gate_hidden = jax.nn.gelu(jnp.dot(gate_in.T, coords, precision=precise) + gate_bias[:, None])
    gate_share = jax.nn.softmax(jnp.dot(gate_out, gate_hidden, precision=precise), axis=0)
    hidden = jax.nn.gelu(
        jnp.einsum("rd,edh->erh", normed, w_in, precision=precise) + b_in[:, None, :]
    )
    outputs = jnp.einsum("erh,ehd->erd", hidden, w_out, precision=precise) + b_out[:, None, :]
    return stream + jnp.einsum("er,erd->rd", gate_share, outputs, precision=precise)


def self_summary(normed, key_weight, value_weight):
    key_soft = head_softmax(jnp.dot(normed, key_weight, precision=precise))
    values = jnp.dot(normed, value_weight, precision=precise).reshape(key_soft.shape)
    return (
        jnp.einsum("rha,rhb->hab", key_soft, values, precision=precise),
        jnp.sum(key_soft, axis=0),
    )


def self_output(stream, normed, query_weight, out_weight, summary, totals):
    queries = head_softmax(jnp.dot(normed, query_weight, precision=precise))
    numerator = jnp.einsum("rha,hab->rhb", queries, summary, precision=precise)
    denominator = jnp.einsum("rha,ha->rh", queries, totals, precision=precise)
    attended = (numerator / denominator[..., None]).reshape(stream.shape)
    return stream + jnp.dot(attended, out_weight, precision=precise)


def per_device(
    query_feats,
    query_coords,
    func_feats,
    func_counts,
    func_present,
    attn_proj,
    attn_out,
    norm_gain,
    norm_bias,
    exp_w_in,
    exp_b_in,
    exp_w_out,
    exp_b_out,
    gate_w_in,
    gate_b_in,
    gate_w_out,
    out_cot,
):
    weights = (
        attn_proj,
        attn_out,
        norm_gain,
        norm_bias,
        exp_w_in,
        exp_b_in,
        exp_w_out,
        exp_b_out,
        gate_w_in,
        gate_b_in,
        gate_w_out,
    )
    shard_rows = func_feats.shape[1]
    positions = lax.axis_index("fn") * shard_rows + jnp.arange(shard_rows, dtype=jnp.int32)
    row_mask = (positions[None, :] < func_counts[:, None]).astype(jnp.float32)
    present = func_present.astype(jnp.float32)
    func_share = present / jnp.sum(present)

    def expert_params(layer_index, expert_set):
        slot = 2 + 2 * expert_set
        return (
            norm_gain[layer_index, slot],
            norm_bias[layer_index, slot],
            exp_w_in[layer_index, expert_set],
            exp_b_in[layer_index, expert_set],
            exp_w_out[layer_index, expert_set],
            exp_b_out[layer_index, expert_set],
            gate_w_in[layer_index, expert_set],
            gate_b_in[layer_index, expert_set],
            gate_w_out[layer_index, expert_set],
        )

    def run_experts(stream_in, *params):
        return expert_block(stream_in, query_coords, *params)

    def expert_back(layer_index, stream_at, expert_set, cotangent, grads):
        result, pullback = jax.vjp(run_experts, stream_at, *expert_params(layer_index, expert_set))
        pieces = pullback(cotangent)
        slot = 2 + 2 * expert_set
        grads[2] = grads[2].at[slot].add(pieces[1])
        grads[3] = grads[3].at[slot].add(pieces[2])
        for position in range(4, 11):
            grads[position] = grads[position].at[expert_set].add(pieces[position - 1])
        return pieces[0]

    stream = query_feats
    kept_states = []
    for layer_index in range(LAYERS):
        part_summary, part_totals = function_summary(
            func_feats,
            row_mask,
            attn_proj[layer_index, 0, 1],
            attn_proj[layer_index, 0, 2],
            norm_gain[layer_index, 1],
            norm_bias[layer_index, 1],
        )
        cross_summary, cross_totals = lax.psum((part_summary, part_totals), "fn")
        stream_cross = cross_block(
            stream,
            attn_proj[layer_index, 0, 0],
            attn_out[layer_index, 0],
            norm_gain[layer_index, 0],
            norm_bias[layer_index, 0],
            cross_summary,
            cross_totals,
            func_share,
        )
        stream_mid = run_experts(stream_cross, *expert_params(layer_index, 0))
        normed = layer_norm(stream_mid, norm_gain[layer_index, 3], norm_bias[layer_index, 3])
        self_part, self_part_tot = self_summary(
            normed, attn_proj[layer_index, 1, 1], attn_proj[layer_index, 1, 2]
        )
        self_sum, self_tot = lax.psum((self_part, self_part_tot), ("pts", "fn"))
        stream_self = self_output(
            stream_mid,
            normed,
            attn_proj[layer_index, 1, 0],
            attn_out[layer_index, 1],
            self_sum,
            self_tot,
        )
        kept_states.append(
            (
                stream,
                stream_cross,
                stream_mid,
                stream_self,
                normed,
                cross_summary,
                cross_totals,
                self_sum,
                self_tot,
            )
        )
        stream = run_experts(stream_self, *expert_params(layer_index, 1))
    upstream = out_cot
    func_rows_grad = jnp.zeros_like(func_feats)
    layer_grads = []
    func_side = []
    for layer_index in reversed(range(LAYERS)):
        (
            stream_in,
            stream_cross,
            stream_mid,
            stream_self,
            normed,
            cross_summary,
            cross_totals,
            self_sum,
            self_tot,
        ) = kept_states[layer_index]
        grads = [jnp.zeros_like(weight[layer_index]) for weight in weights]
        upstream = expert_back(layer_index, stream_self, 1, upstream, grads)
        result, pullback = jax.vjp(
            self_output,
            stream_mid,
            normed,
            attn_proj[layer_index, 1, 0],
            attn_out[layer_index, 1],
            self_sum,
            self_tot,
        )
        grad_stream, grad_normed, grad_query, grad_out, grad_sum, grad_tot = pullback(upstream)
        grad_sum, grad_tot = lax.psum((grad_sum, grad_tot), ("pts", "fn"))
        result, pullback = jax.vjp(
            self_summary, normed, attn_proj[layer_index, 1, 1], attn_proj[layer_index, 1, 2]
        )
        grad_normed_more, grad_key, grad_value = pullback((grad_sum, grad_tot))
        result, pullback = jax.vjp(
            layer_norm, stream_mid, norm_gain[layer_index, 3], norm_bias[layer_index, 3]
        )
        grad_stream_more, grad_gain, grad_bias = pullback(grad_normed + grad_normed_more)
        upstream = grad_stream + grad_stream_more
        grads[0] = grads[0].at[1].set(jnp.stack([grad_query, grad_key, grad_value]))
        grads[1] = grads[1].at[1].set(grad_out)
        grads[2] = grads[2].at[3].add(grad_gain)
        grads[3] = grads[3].at[3].add(grad_bias)
        upstream = expert_back(layer_index, stream_cross, 0, upstream, grads)

        def cross_local(stream_at, query_weight, out_weight, gain_vec, bias_vec, summary, totals):
            return cross_block(
                stream_at, query_weight, out_weight, gain_vec, bias_vec, summary, totals, func_share
            )

        result, pullback = jax.vjp(
            cross_local,
            stream_in,
            attn_proj[layer_index, 0, 0],
            attn_out[layer_index, 0],
            norm_gain[layer_index, 0],
            norm_bias[layer_index, 0],
            cross_summary,
            cross_totals,
        )
        upstream, grad_query, grad_out, grad_gain, grad_bias, grad_sum, grad_tot = pullback(
            upstream
        )
        grad_sum, grad_tot = lax.psum((grad_sum, grad_tot), ("pts", "fn"))

        def func_local(rows_at, key_weight, value_weight, gain_vec, bias_vec):
            return function_summary(rows_at, row_mask, key_weight, value_weight, gain_vec, bias_vec)

        result, pullback = jax.vjp(
            func_local,
            func_feats,
            attn_proj[layer_index, 0, 1],
            attn_proj[layer_index, 0, 2],
            norm_gain[layer_index, 1],
            norm_bias[layer_index, 1],
        )
        grad_rows, grad_key, grad_value, grad_fgain, grad_fbias = pullback((grad_sum, grad_tot))
        func_rows_grad = func_rows_grad + grad_rows
        grads[0] = grads[0].at[0, 0].set(grad_query)
        grads[1] = grads[1].at[0].set(grad_out)
        grads[2] = grads[2].at[0].add(grad_gain)
        grads[3] = grads[3].at[0].add(grad_bias)
        func_side.append((jnp.stack([grad_key, grad_value]), grad_fgain, grad_fbias))
        layer_grads.append(grads)
    layer_grads = layer_grads[::-1]
    stacked = [
        jnp.stack([layer_entry[position] for layer_entry in layer_grads]) for position in range(11)
    ]
    stacked = list(
        lax.psum(
            (
                stacked[0],
                stacked[1],
                stacked[2],
                stacked[3],
                stacked[4],
                stacked[5],
                stacked[6],
                stacked[7],
                stacked[8],
                stacked[9],
                stacked[10],
            ),
            ("pts", "fn"),
        )
    )
    func_side = func_side[::-1]
    func_proj = jnp.stack([layer_entry[0] for layer_entry in func_side])
    func_gain = jnp.stack([layer_entry[1] for layer_entry in func_side])
    func_bias = jnp.stack([layer_entry[2] for layer_entry in func_side])
    func_proj, func_gain, func_bias = lax.psum((func_proj, func_gain, func_bias), "fn")
    stacked[0] = stacked[0].at[:, 0, 1:3].add(func_proj)
    stacked[2] = stacked[2].at[:, 1].add(func_gain)
    stacked[3] = stacked[3].at[:, 1].add(func_bias)
    return (
        stream,
        upstream,
        func_rows_grad,
        stacked[0],
        stacked[1],
        stacked[2],
        stacked[3],
        stacked[4],
        stacked[5],
        stacked[6],
        stacked[7],
        stacked[8],
        stacked[9],
        stacked[10],
    )


def solution(mesh):
    return jax.shard_map(
        per_device,
        mesh=mesh,
        in_specs=(
            P(("pts", "fn"), None),
            P(None, ("pts", "fn")),
            P(None, "fn", None),
            P(),
            P(),
            P(),
            P(),
            P(),
            P(),
            P(),
            P(),
            P(),
            P(),
            P(),
            P(),
            P(),
            P(("pts", "fn"), None),
        ),
        out_specs=(
            P(("pts", "fn"), None),
            P(("pts", "fn"), None),
            P(None, "fn", None),
            P(),
            P(),
            P(),
            P(),
            P(),
            P(),
            P(),
            P(),
            P(),
            P(),
            P(),
        ),
        check_vma=False,
    )
```

profile of v0, /device:TPU:0, one launch (start us, length us, event | category | flops | bytes accessed | tf_op | source)
XLA Modules:
  0.0 950.8 jit_solution(7316311715836901562)
XLA Ops:
  51.7 29.6 %all-reduce.29 = (f32[3,8,16,16]{3,2,1,0:T(8,128)}, f32[3,8,16]{2,0,1:T(4,128)S(1)}, f32[3,8,16,16]{3,2,1,0:T(8,128)}, f32[3,8,16]{2,0,1:T(4,128)}) all-reduce(f32[3,8,16,16]{3,2,1,0:T(8,128)S(1)} %fusion.587, f32[3,8,16]{2,0,1:T(4,128)S(1)} %copy.237, f32[3,8,16,16]{3,2,1,0:T(8,128)S(1)} %fusion.589, ...), channel_id=1, replica_groups=mesh['pts'=8,'fn'=4] {'fn'}, use_global_device_ids=true, to_apply=%region_4.0 | all-reduce | flops 13056 | bytes 104448 | tf_op jit(solution)/shard_map/psum | solution.py:154
  95.9 7.7 multiply_reduce_fusion.6
  114.1 40.0 %all-reduce.26 = (f32[8,16,16]{2,1,0:T(8,128)}, f32[8,16]{1,0:T(8,128)S(1)}) all-reduce(f32[8,16,16]{2,1,0:T(8,128)} %fusion.582, f32[8,16]{1,0:T(8,128)S(1)} %fusion.581), channel_id=1, replica_groups=mesh['pts'=8,'fn'=4] {'pts','fn'}, use_global_device_ids=true, to_apply=%region_20.0 | all-reduce | flops 2176 | bytes 17408 | tf_op jit(solution)/shard_map/psum | solution.py:170
  169.8 7.6 multiply_reduce_fusion.5
  196.8 7.7 multiply_reduce_fusion.4
  217.8 41.8 %all-reduce.25 = (f32[8,16,16]{2,1,0:T(8,128)}, f32[8,16]{1,0:T(8,128)}) all-reduce(f32[8,16,16]{2,1,0:T(8,128)} %fusion.585, f32[8,16]{1,0:T(8,128)} %fusion.584), channel_id=1, replica_groups=mesh['pts'=8,'fn'=4] {'pts','fn'}, use_global_device_ids=true, to_apply=%region_46.0 | all-reduce | flops 2176 | bytes 17408 | tf_op jit(solution)/shard_map/psum | solution.py:170
  282.3 11.2 %fusion.108 = f32[1024,1,4]{2,1,0:T(1,128)} fusion(f32[1024,128,1]{1,2,0:T(1,128)S(1)} %bitcast.1206, f32[4,1024,128]{2,1,0:T(8,128)S(1)} %convolution_add_fusion), kind=kOutput, calls=%fused_computation.157 | convolution fusion | flops 6291456 | bytes 2637824 | tf_op jit(solution)/shard_map/transpose(jvp(er,erd->rd))/dot_general | solution.py:58
  304.5 9.5 fusion.41
  316.0 7.0 fusion.618
  334.9 40.0 %all-reduce.24 = (f32[8,16,16]{2,1,0:T(8,128)S(1)}, f32[8,16]{1,0:T(8,128)S(1)}) all-reduce(f32[8,16,16]{2,1,0:T(8,128)S(1)} %fusion.393, f32[8,16]{1,0:T(8,128)S(1)} %bitcast.1237), channel_id=1, replica_groups=mesh['pts'=8,'fn'=4] {'pts','fn'}, use_global_device_ids=true, to_apply=%region_59.0 | all-reduce | flops 2176 | bytes 17408 | tf_op jit(solution)/shard_map/psum | solution.py:221
  391.2 9.7 %fusion.47 = (f32[4,256,1024]{1,2,0:T(8,128)S(1)}, f32[4,1024,256]{2,1,0:T(8,128)}) fusion(f32[1024,4,256]{2,0,1:T(8,128)} %copy-done.13, f32[4,256]{1,0:T(4,128)S(1)} %copy-done.258, f32[2,2,4,256,128]{4,3,2,1,0:T(8,128)} %param.138, f32[1024,4]{0,1:T(4,128)S(1)} %copy-done.184, f32[1024,128]{1,0:T(8,128)} %copy.270), kind=kOutput, calls=%fused_computation.63 | convolution fusion | flops 1632108544 | bytes 13651968 | tf_op jit(solution)/shard_map/transpose(jvp(erh,ehd->erd))/dot_general | solution.py:57
  446.7 8.7 fusion.53
  473.7 41.2 %all-reduce.23 = (f32[8,16,16]{2,1,0:T(8,128)S(1)}, f32[8,16]{1,0:T(8,128)}) all-reduce(f32[8,16,16]{2,1,0:T(8,128)S(1)} %fusion.394, f32[8,16]{1,0:T(8,128)S(1)} %bitcast.1238), channel_id=1, replica_groups=mesh['pts'=8,'fn'=4] {'pts','fn'}, use_global_device_ids=true, to_apply=%region_74.0 | all-reduce | flops 2176 | bytes 17408 | tf_op jit(solution)/shard_map/psum | solution.py:221
  531.1 9.7 %fusion.59 = (f32[4,256,1024]{1,2,0:T(8,128)S(1)}, f32[4,1024,256]{2,1,0:T(8,128)}) fusion(f32[1024,4,256]{2,0,1:T(8,128)} %copy-done.7, f32[4,256]{1,0:T(4,128)S(1)} %copy-done.255, f32[2,2,4,256,128]{4,3,2,1,0:T(8,128)} %param.138, f32[1024,4]{0,1:T(4,128)S(1)} %copy-done.181, f32[1024,128]{1,0:T(8,128)} %copy.282), kind=kOutput, calls=%fused_computation.75 | convolution fusion | flops 1632108544 | bytes 13651968 | tf_op jit(solution)/shard_map/transpose(jvp(erh,ehd->erd))/dot_general | solution.py:57
  610.4 10.7 %fusion.141 = f32[1,4,256,128]{3,2,1,0:T(8,128)S(1)} fusion(f32[1024,4,256]{2,0,1:T(8,128)} %copy-done.16, f32[4,256]{1,0:T(4,128)S(1)} %copy-done.266, f32[1024,4]{0,1:T(4,128)S(1)} %get-tuple-element.810, f32[1024,128]{1,0:T(8,128)} %param.143), kind=kOutput, calls=%fused_computation.193 | convolution fusion | flops 1620574208 | bytes 5263360 | tf_op jit(solution)/shard_map/transpose(jvp(erh,ehd->erd))/dot_general | solution.py:57
  630.7 8.4 fusion.150
  639.3 6.8 convolution_bitcast_fusion.9
  649.2 8.3 fusion.147
  657.7 7.1 fusion.173
  666.4 8.4 fusion.156
  693.8 50.4 %all-reduce.36.cloned.1.call-done = (f32[3,8,16,16]{2,3,0,1:T(8,128)}, f32[3,8,16]{2,0,1:T(4,128)}, f32[3,8,16,16]{2,3,0,1:T(8,128)}, f32[3,8,16]{2,0,1:T(4,128)...) async-done(((f32[3,8,16,16]{2,3,0,1:T(8,128)}, ...) | async-done | bytes 103440 | tf_op jit(solution)/shard_map/psum | solution.py:255
  763.9 10.8 %all-reduce.28 = (f32[2,1,128]{2,1,0:T(1,128)S(1)}, f32[2,1,128]{2,1,0:T(1,128)S(1)}) all-reduce(f32[2,1,128]{2,1,0:T(1,128)S(1)} %bitcast.1239, f32[2,1,128]{2,1,0:T(1,128)S(1)} %bitcast.1240), channel_id=1, replica_groups=mesh['pts'=8,'fn'=4] {'fn'}, use_global_device_ids=true, to_apply=%region_109.0 | all-reduce | flops 512 | bytes 4096 | tf_op jit(solution)/shard_map/psum | solution.py:302
  789.3 110.5 %all-reduce.38.cloned.1.call-done = (f32[2,2,3,128,128]{4,3,2,1,0:T(8,128)}, f32[2,2,128,128]{3,2,1,0:T(8,128)}, f32[2,2,4,128,256]{3,4,2,1,0:T(8,128)}, f32[2,2,4,256,128]{4,3,2,1,0:T(8,128)}) async-done(((f32[2,2,3,128,128]{4,3,2,1,0:T(8,128)}, f32[2,2,128,128]{3,2,1,0:T(8,128)}, f32[2,2,4,128,256]{3,4,2,1,0:T(8,128)}, f32[2,2,4,256,128]{4,3,2,1,0:T(8,128)}), (f32[2,2,3,128,128]{4,3,2,1,0:T(8,128)}, ...) | async-done | bytes 5242896 | tf_op jit(solution)/shard_map/psum | solution.py:281
  902.8 33.7 %all-reduce.34.cloned.1.call-done = f32[2,1,2,128,128]{4,3,2,1,0:T(8,128)} async-done(((f32[2,1,2,128,128]{4,3,2,1,0:T(8,128)}), f32[2,1,2,128,128]{4,3,2,1,0:T(8,128)}) %all-reduce.34.cloned.1.call-update) | async-done | bytes 262160 | tf_op jit(solution)/shard_map/psum | solution.py:302
  (1123 shorter events, 404.7 us)
Async XLA Ops:
  7.2 737.0 %all-reduce.36.cloned.1.call-start = ((), (), s32[]{:S(2)}) async-start(), calls=%async_computation.1 | async-start | bytes 970752 | tf_op jit(solution)/shard_map/psum | solution.py:255
  23.4 84.9 %copy-start.191 = (f32[128]{0:T(128)}, f32[128]{0:T(128)S(1)}, u32[]{:S(2)}) copy-start(f32[128]{0:T(128)S(1)} %get-tuple-element.830) | copy-start | bytes 1540
  34.7 47.7 %copy-start.49 = (f32[1024,8,16]{0,2,1:T(8,128)}, f32[1024,8,16]{0,2,1:T(8,128)S(1)}, u32[]{:S(2)}) copy-start(f32[1024,8,16]{0,2,1:T(8,128)S(1)} %get-tuple-element.856) | copy-start | bytes 1572868
  49.0 32.3 %copy-start.28 = (f32[3,512,8,16]{1,3,2,0:T(8,128)}, f32[3,512,8,16]{1,3,2,0:T(8,128)S(1)}, u32[]{:S(2)}) copy-start(f32[3,512,8,16]{1,3,2,0:T(8,128)S(1)} %get-tuple-element.852) | copy-start | bytes 2359300
  104.0 50.5 %copy-start.201 = (f32[1024]{0:T(1024)}, f32[1024]{0:T(1024)S(1)}, u32[]{:S(2)}) copy-start(f32[1024]{0:T(1024)S(1)} %multiply_reduce_fusion.43) | copy-start | bytes 12292
  104.8 49.7 %copy-start.95 = (f32[1024,8,16]{0,2,1:T(8,128)}, f32[1024,8,16]{0,2,1:T(8,128)S(1)}, u32[]{:S(2)}) copy-start(f32[1024,8,16]{0,2,1:T(8,128)S(1)} %fusion.300) | copy-start | bytes 1572868
  107.6 56.7 %copy-start.87 = (f32[1024,8,16]{0,2,1:T(8,128)}, f32[1024,8,16]{0,2,1:T(8,128)S(1)}, u32[]{:S(2)}) copy-start(f32[1024,8,16]{0,2,1:T(8,128)S(1)} %get-tuple-element.868) | copy-start | bytes 1572868
  107.6 56.7 %copy-start.129 = (f32[1024,8]{0,1:T(8,128)}, f32[1024,8]{0,1:T(8,128)S(1)}, u32[]{:S(2)}) copy-start(f32[1024,8]{0,1:T(8,128)S(1)} %get-tuple-element.867) | copy-start | bytes 98308
  111.9 52.4 %copy-start.37 = (f32[1024,8,16]{0,2,1:T(8,128)}, f32[1024,8,16]{0,2,1:T(8,128)S(1)}, u32[]{:S(2)}) copy-start(f32[1024,8,16]{0,2,1:T(8,128)S(1)} %get-tuple-element.866) | copy-start | bytes 1572868
  114.1 51.0 %copy-start.248 = (f32[128]{0:T(128)S(1)}, f32[128]{0:T(128)}, u32[]{:S(2)}) copy-start(f32[128]{0:T(128)} %get-tuple-element.829) | copy-start | bytes 1540
  332.5 44.2 %copy-start.162 = (f32[1024,8]{0,1:T(8,128)S(1)}, f32[1024,8]{0,1:T(8,128)}, u32[]{:S(2)}) copy-start(f32[1024,8]{0,1:T(8,128)} %multiply_divide_fusion.9) | copy-start | bytes 98308
  471.3 45.5 %copy-start.160 = (f32[1024,8]{0,1:T(8,128)S(1)}, f32[1024,8]{0,1:T(8,128)}, u32[]{:S(2)}) copy-start(f32[1024,8]{0,1:T(8,128)} %multiply_divide_fusion.5) | copy-start | bytes 98308
  610.3 289.5 %all-reduce.38.cloned.1.call-start = ((), (), s32[]{:S(2)}) async-start(), calls=%async_computation.2 | async-start | bytes 10485760 | tf_op jit(solution)/shard_map/psum | solution.py:281
  687.7 57.3 %copy-start.29 = (f32[3,512,8,16]{1,3,2,0:T(8,128)S(1)}, f32[3,512,8,16]{1,3,2,0:T(8,128)}, u32[]{:S(2)}) copy-start(f32[3,512,8,16]{1,3,2,0:T(8,128)} %copy-done.28) | copy-start | bytes 2359300
  687.7 57.3 %copy-start.159 = (f32[3,512]{1,0:T(4,128)S(1)}, f32[3,512]{1,0:T(4,128)}, u32[]{:S(2)}) copy-start(f32[3,512]{1,0:T(4,128)} %copy-done.158) | copy-start | bytes 18436
  687.7 248.8 %all-reduce.34.cloned.1.call-start = ((), (), s32[]{:S(2)}) async-start(), calls=%async_computation | async-start | bytes 524288 | tf_op jit(solution)/shard_map/psum | solution.py:302
  689.6 59.7 %copy-start.27 = (f32[3,512,8,16]{1,3,2,0:T(8,128)S(1)}, f32[3,512,8,16]{1,3,2,0:T(8,128)}, u32[]{:S(2)}) copy-start(f32[3,512,8,16]{1,3,2,0:T(8,128)} %copy-done.26) | copy-start | bytes 2359300
  789.3 151.0 %copy-start.276 = (f32[2,2,4,256]{3,2,1,0:T(4,128)S(1)}, f32[2,2,4,256]{3,2,1,0:T(4,128)}, u32[]{:S(2)}) copy-start(f32[2,2,4,256]{3,2,1,0:T(4,128)} %get-tuple-element.964) | copy-start | bytes 49156
  899.8 36.7 %copy-start.107 = (f32[2,2,3,128,128]{4,3,2,1,0:T(8,128)S(1)}, f32[2,2,3,128,128]{4,3,2,1,0:T(8,128)}, u32[]{:S(2)}) copy-start(f32[2,2,3,128,128]{4,3,2,1,0:T(8,128)} %get-tuple-element.767) | copy-start | bytes 2359300
  899.8 39.8 %copy-start.139 = (f32[2,2,128,128]{3,2,1,0:T(8,128)S(1)}, f32[2,2,128,128]{3,2,1,0:T(8,128)}, u32[]{:S(2)}) copy-start(f32[2,2,128,128]{3,2,1,0:T(8,128)} %get-tuple-element.960) | copy-start | bytes 786436
  899.8 41.1 %copy-start.101 = (f32[2,2,4,256,128]{4,3,2,1,0:T(8,128)S(1)}, f32[2,2,4,256,128]{4,3,2,1,0:T(8,128)}, u32[]{:S(2)}) copy-start(f32[2,2,4,256,128]{4,3,2,1,0:T(8,128)} %get-tuple-element.965) | copy-start | bytes 6291460
  902.8 39.4 %copy-start.296 = (f32[2,2,4,128]{3,2,1,0:T(4,128)S(1)}, f32[2,2,4,128]{3,2,1,0:T(4,128)}, u32[]{:S(2)}) copy-start(f32[2,2,4,128]{3,2,1,0:T(4,128)} %get-tuple-element.966) | copy-start | bytes 24580
  902.8 40.0 %copy-start.329 = (f32[2,2,128]{2,1,0:T(2,128)S(1)}, f32[2,2,128]{2,1,0:T(2,128)}, u32[]{:S(2)}) copy-start(f32[2,2,128]{2,1,0:T(2,128)} %get-tuple-element.968) | copy-start | bytes 6148
  902.8 40.6 %copy-start.295 = (f32[2,2,4,128]{3,2,1,0:T(4,128)S(1)}, f32[2,2,4,128]{3,2,1,0:T(4,128)}, u32[]{:S(2)}) copy-start(f32[2,2,4,128]{3,2,1,0:T(4,128)} %get-tuple-element.969) | copy-start | bytes 24580
  (341 other events, 2474.7 us)
Sparse Core Ops, SparseCore 0:
  610.4 133.6 all-reduce.35
  751.4 148.3 all-reduce.37
  902.7 33.7 all-reduce.33
where the time goes:
time: 960 us; the launch traced here: 951 us
  matrix products  341 us (36%)
  blocking collectives  203 us (21%)
  waiting for transfers between devices  195 us (20%)
  other arithmetic  117 us (12%)
  local copies, waits for them, and re-layouts  74.4 us (8%)
  between operations  19.7 us (2%)
    psum x1, waiting for transfers between devices, per_device(): lax.psum((stacked[0], stacked[1], stacked[2], stacked[3], stacked[4], sta...  111 us
    dot_general x12, matrix products, expert_block(): jnp.einsum('erh,ehd->erd', hidden, w_out, precision=precise)  103 us
    psum x2, blocking collectives, per_device(): self_sum, self_tot = lax.psum((self_part, self_part_tot), ('pts', 'fn'))  81.8 us
    psum x2, blocking collectives, per_device(): grad_sum, grad_tot = lax.psum((grad_sum, grad_tot), ('pts', 'fn'))  81.2 us
    dot_general x12, matrix products, expert_block(): jnp.einsum('rd,edh->erh', normed, w_in, precision=precise)  70.3 us
    psum x1, waiting for transfers between devices, per_device(): grad_sum, grad_tot = lax.psum((grad_sum, grad_tot), ('pts', 'fn'))  50.4 us
    psum x1, waiting for transfers between devices, per_device(): lax.psum((func_proj, func_gain, func_bias), 'fn')  33.7 us
    unnamed x739, local copies, waits for them, and re-layouts  31.2 us
  transfers between devices with their start and end apart: 3, of which 3 were waited for; matrix products, arithmetic and copies ran while one was open for 12% of the time, Pallas kernels for 0%

commit v1 on v0

v1 whole, which is shorter than its diff:
```python
import math
from types import SimpleNamespace

import jax
import jax.numpy as jnp
from jax import lax
from jax.experimental import pallas as pl
from jax.experimental.pallas import tpu as pltpu
from jax.sharding import PartitionSpec as P

D = 128
HEADS = 8
HEAD_SIZE = 16
FH = 256
EXPERTS = 4
HID = EXPERTS * FH
NF = 3
LAYERS = 2
GROUP = 8

f32, bf16 = jnp.float32, jnp.bfloat16
CHUNK = 128
MESH = pl.DeviceIdType.MESH


def split(v):
    hi = v.astype(bf16)
    return hi, (v - hi.astype(f32)).astype(bf16)


def join(hi, lo):
    return hi.astype(f32) + lo.astype(f32)


def dot(a, b, ca, cb):
    return lax.dot_general(a, b, (((ca,), (cb,)), ((), ())), preferred_element_type=f32)


def nn(a, b):
    return dot(a, b, 1, 0)


def tn(a, b):
    return dot(a, b, 0, 0)


def nt(a, b):
    return dot(a, b, 1, 1)


def k3(hi, lo):
    return jnp.concatenate([hi, hi, lo], axis=0)


def nn_rows(w_ref, at, hi, lo):
    both = nn(w_ref[at + (slice(0, 256),)], hi)
    return both[:128] + both[128:] + nn(w_ref[at + (slice(0, 128),)], lo)


def nt_pair(a_hi, a_lo, b_both, b_hi):
    wide = nt(a_hi, b_both)
    n = b_hi.shape[0]
    return wide[:, :n] + wide[:, n:] + nt(a_lo, b_hi)


def normalise(v):
    average = jnp.mean(v, axis=0, keepdims=True)
    centred = v - average
    variance = jnp.mean(centred * centred, axis=0, keepdims=True)
    scale = lax.rsqrt(variance + 1e-05)
    return centred * scale, scale


def norm_back(d_normed, gain_col, unit, scale):
    d_unit = d_normed * gain_col
    first = jnp.mean(d_unit, axis=0, keepdims=True)
    second = jnp.mean(d_unit * unit, axis=0, keepdims=True)
    return scale * (d_unit - first - unit * second)


def by_head(v):
    return v.reshape(HEADS, HEAD_SIZE, v.shape[1])


def head_softmax(v):
    shaped = by_head(v)
    top = jnp.max(shaped, axis=1, keepdims=True)
    power = jnp.exp(shaped - top)
    total = jnp.sum(power, axis=1, keepdims=True)
    return (power * (1.0 / total)).reshape(v.shape)


def head_softmax_back(soft, d_soft):
    total = jnp.sum(by_head(soft * d_soft), axis=1, keepdims=True)
    return (by_head(soft) * (by_head(d_soft) - total)).reshape(soft.shape)


def head_rows(v):
    total = jnp.sum(by_head(v), axis=1, keepdims=True)
    return jnp.concatenate([total[h] for h in range(HEADS)], axis=0)


def head_spread(rows):
    return jnp.concatenate(
        [jnp.broadcast_to(rows[h : h + 1], (HEAD_SIZE, rows.shape[1])) for h in range(HEADS)], axis=0
    )


C1 = 0.7978845608028654
C2 = C1 * 0.044715


def gelu_both(v):
    square = v * v
    gate = 0.5 + 0.5 * jnp.tanh(v * (C1 + C2 * square))
    value = v * gate
    slope = gate + value * (1.0 - gate) * (2.0 * C1 + 6.0 * C2 * square)
    return value, slope


def fold_lanes(v):
    total = v[:, :128]
    for start in range(128, v.shape[1], 128):
        total = total + v[:, start : start + 128]
    return total


def row_sum(folded):
    return jnp.sum(folded.T, axis=0, keepdims=True)


def head_masks():
    rows = lax.broadcasted_iota(jnp.int32, (D, D), 0) // HEAD_SIZE
    cols = lax.broadcasted_iota(jnp.int32, (D, D), 1) // HEAD_SIZE
    square = jnp.where(rows == cols, 1.0, 0.0).astype(f32)
    heads = lax.broadcasted_iota(jnp.int32, (HEADS, D), 0)
    cols8 = lax.broadcasted_iota(jnp.int32, (HEADS, D), 1) // HEAD_SIZE
    return square, jnp.where(heads == cols8, 1.0, 0.0).astype(f32)


def pack_summary(square_part, total_row, square):
    compact = jnp.sum((square_part * square).reshape(HEADS, HEAD_SIZE, D), axis=0)
    return jnp.concatenate([compact, total_row, jnp.zeros((7, D), f32)], axis=0)


def unpack_summary(block, square):
    spread = jnp.concatenate([block[:HEAD_SIZE]] * HEADS, axis=0) * square
    return spread, block[HEAD_SIZE : HEAD_SIZE + 1]


class Exchange:
    def __init__(self, stages, slots, sends, receives):
        self.stages, self.slots, self.sends, self.receives = stages, slots, sends, receives

    @staticmethod
    def place(stage):
        axis, stride, size = stage
        index = lax.axis_index(axis)
        digit = lax.rem(lax.div(index, stride), size)
        return axis, index - digit * stride, digit

    @staticmethod
    def member(stage, offset):
        axis, stride, size = stage
        axis, base, digit = Exchange.place(stage)
        other = lax.rem(digit + offset, size)
        return other, {axis: base + other * stride}

    def copy(self, n, offset, arriving=False):
        stage = self.stages[n]
        _, _, digit = self.place(stage)
        other, device = self.member(stage, offset)
        place = other if arriving else digit
        return pltpu.make_async_remote_copy(
            src_ref=self.slots[n].at[place],
            dst_ref=self.slots[n].at[place],
            send_sem=self.sends[n].at[offset],
            recv_sem=self.receives[n].at[place],
            device_id=device,
            device_id_type=MESH,
        )

    def start(self, n, value):
        _, _, digit = self.place(self.stages[n])
        self.slots[n][digit] = value
        for offset in range(1, self.stages[n][2]):
            self.copy(n, offset).start()

    def finish(self, n):
        size = self.stages[n][2]
        for offset in range(1, size):
            self.copy(n, offset, True).wait_recv()
        total = self.slots[n][0]
        for place in range(1, size):
            total = total + self.slots[n][place]
        for offset in range(1, size):
            self.copy(n, offset).wait_send()
        return total

    def finish_all(self, n=0):
        while True:
            total = self.finish(n)
            n += 1
            if n == len(self.stages):
                return total
            self.start(n, total)


class Reduction:
    def __init__(self, buffers, total, rows, first, n_pts, n_fn):
        self.r = SimpleNamespace(**buffers)
        self.total, self.first = total, first
        self.plane, self.n_fn = n_pts // 2, n_fn
        self.half = rows // 2
        self.part = self.half // self.plane
        self.deep = self.part % (8 * n_fn) == 0
        self.last = self.part // n_fn if self.deep else self.part
        index, self.z = lax.axis_index("pts"), lax.axis_index("fn")
        self.core, self.q = lax.rem(index, 2), lax.div(index, 2)
        self.steps = [self.add_pair, self.add_plane, self.add_fn, self.spread_plane, self.spread_pair, self.end]
        pair, plane, fn = 1.5 + rows / 700, 3.5 + rows / 160, 4.5 + rows / 320
        self.waits = [pair, plane, fn, fn if self.deep else 0.5, plane + 0.5, pair + 0.5]

    @staticmethod
    def scratch(rows, n_pts, n_fn):
        plane = n_pts // 2
        part = max(rows // (2 * plane), 1)
        last = part // n_fn if part % (8 * n_fn) == 0 else part
        dma = pltpu.SemaphoreType.DMA
        return dict(
            stage=pltpu.VMEM((rows, 256), f32),
            pair=pltpu.VMEM((rows // 2, 256), f32),
            planes=pltpu.VMEM((plane, part, 256), f32),
            fns=pltpu.VMEM((n_fn, last, 256), f32),
            pair_sems=dma((2,)),
            plane_sends=dma((plane,)),
            plane_receives=dma((plane,)),
            fn_sends=dma((n_fn,)),
            fn_receives=dma((n_fn,)),
            out_pair_sems=dma((2,)),
            out_plane_sends=dma((plane,)),
            out_plane_receives=dma((plane,)),
            out_fn_sends=dma((n_fn,)),
            out_fn_receives=dma((n_fn,)),
            local_sem=dma((1,)),
        )

    @staticmethod
    def remote(src, dst, send, receive, device):
        return pltpu.make_async_remote_copy(
            src_ref=src, dst_ref=dst, send_sem=send, recv_sem=receive, device_id=device, device_id_type=MESH
        )

    def rows(self, start, count):
        return pl.ds(pl.multiple_of(start, 8), count)

    def own_part(self):
        return self.core * self.half + self.q * self.part

    def own_last(self):
        return self.own_part() + (self.z * self.last if self.deep else 0)

    def in_total(self, start, count):
        return self.total.at[self.rows(self.first + start, count)]

    def pair_copy(self):
        away = self.r.stage.at[self.rows((1 - self.core) * self.half, self.half)]
        sems = self.r.pair_sems
        device = {"pts": 2 * self.q + 1 - self.core}
        return self.remote(away, self.r.pair.at[pl.ds(0, self.half)], sems.at[0], sems.at[1], device)

    def plane_copy(self, offset, arriving=False):
        other = lax.rem(self.q + offset, self.plane)
        src = self.r.stage.at[self.rows(self.core * self.half + other * self.part, self.part)]
        slot = other if arriving else self.q
        return self.remote(
            src,
            self.r.planes.at[slot, pl.ds(0, self.part)],
            self.r.plane_sends.at[offset],
            self.r.plane_receives.at[slot],
            {"pts": 2 * other + self.core},
        )

    def fn_copy(self, offset, arriving=False):
        other = lax.rem(self.z + offset, self.n_fn)
        start = self.own_part() + (other * self.last if self.deep else 0)
        slot = other if arriving else self.z
        return self.remote(
            self.r.stage.at[self.rows(start, self.last)],
            self.r.fns.at[slot, pl.ds(0, self.last)],
            self.r.fn_sends.at[offset],
            self.r.fn_receives.at[slot],
            {"fn": other},
        )

    def local_copy(self):
        src = self.r.stage.at[self.rows(self.own_last(), self.last)]
        return pltpu.make_async_copy(src, self.in_total(self.own_last(), self.last), self.r.local_sem.at[0])

    def out_fn_copy(self, offset, arriving=False):
        other = lax.rem(self.z + offset, self.n_fn)
        place = other if arriving else self.z
        src = self.r.stage.at[self.rows(self.own_last(), self.last)]
        return self.remote(
            src,
            self.in_total(self.own_part() + place * self.last, self.last),
            self.r.out_fn_sends.at[offset],
            self.r.out_fn_receives.at[place],
            {"fn": other},
        )

    def out_plane_copy(self, offset, arriving=False):
        other = lax.rem(self.q + offset, self.plane)
        place = other if arriving else self.q
        region = self.in_total(self.core * self.half + place * self.part, self.part)
        return self.remote(
            region,
            region,
            self.r.out_plane_sends.at[offset],
            self.r.out_plane_receives.at[place],
            {"pts": 2 * other + self.core},
        )

    def out_pair_copy(self, arriving=False):
        place = 1 - self.core if arriving else self.core
        region = self.in_total(place * self.half, self.half)
        sems = self.r.out_pair_sems
        return self.remote(region, region, sems.at[0], sems.at[1], {"pts": 2 * self.q + 1 - self.core})

    def begin(self):
        self.pair_copy().start()

    def step(self):
        self.steps.pop(0)()

    def add_pair(self):
        self.pair_copy().wait()
        mine = self.rows(self.core * self.half, self.half)
        self.r.stage[mine, :] += self.r.pair[0 : self.half, :]
        for offset in range(1, self.plane):
            self.plane_copy(offset).start()

    def add_plane(self):
        mine = self.rows(self.own_part(), self.part)
        sums = self.r.stage[mine, :]
        for offset in range(1, self.plane):
            self.plane_copy(offset, True).wait_recv()
            sums = sums + self.r.planes[lax.rem(self.q + offset, self.plane), 0 : self.part, :]
        self.r.stage[mine, :] = sums
        for offset in range(1, self.plane):
            self.plane_copy(offset).wait_send()
        for offset in range(1, self.n_fn):
            self.fn_copy(offset).start()

    def add_fn(self):
        mine = self.rows(self.own_last(), self.last)
        self.r.fns[self.z, 0 : self.last, :] = self.r.stage[mine, :]
        for offset in range(1, self.n_fn):
            self.fn_copy(offset, True).wait_recv()
        for offset in range(1, self.n_fn):
            self.fn_copy(offset).wait_send()
        sums = self.r.fns[0, 0 : self.last, :]
        for place in range(1, self.n_fn):
            sums = sums + self.r.fns[place, 0 : self.last, :]
        self.r.stage[mine, :] = sums
        self.local_copy().start()
        if self.deep:
            for offset in range(1, self.n_fn):
                self.out_fn_copy(offset).start()

    def spread_plane(self):
        self.local_copy().wait()
        if self.deep:
            for offset in range(1, self.n_fn):
                self.out_fn_copy(offset, True).wait_recv()
            for offset in range(1, self.n_fn):
                self.out_fn_copy(offset).wait_send()
        for offset in range(1, self.plane):
            self.out_plane_copy(offset).start()

    def spread_pair(self):
        for offset in range(1, self.plane):
            self.out_plane_copy(offset, True).wait_recv()
        for offset in range(1, self.plane):
            self.out_plane_copy(offset).wait_send()
        self.out_pair_copy().start()

    def end(self):
        self.out_pair_copy().wait_send()
        self.out_pair_copy(True).wait_recv()


class SharedReduction:
    def __init__(self, buffers, total, n_pts, n_fn):
        self.r = SimpleNamespace(**buffers)
        self.total, self.n_pts, self.n_fn = total, n_pts, n_fn
        self.part = self.r.stage.shape[0] // n_pts
        self.p, self.z = lax.axis_index("pts"), lax.axis_index("fn")
        self.steps = [self.add, self.end]
        self.waits = [5.0, 5.0]

    @staticmethod
    def scratch(rows, n_pts, n_fn):
        dma = pltpu.SemaphoreType.DMA
        return dict(
            stage=pltpu.VMEM((rows, D), f32),
            slots=pltpu.VMEM((n_fn, rows // n_pts, D), f32),
            fn_sends=dma((n_fn,)),
            fn_receives=dma((n_fn,)),
            sends=dma((n_pts,)),
            receives=dma((n_pts,)),
            local_sem=dma((1,)),
        )

    def mine(self, place):
        return pl.ds(pl.multiple_of(place * self.part, 8), self.part)

    def fn_copy(self, offset, arriving=False):
        other = lax.rem(self.z + offset, self.n_fn)
        slot = other if arriving else self.z
        src, dst = self.r.stage.at[self.mine(self.p)], self.r.slots.at[slot]
        return Reduction.remote(
            src, dst, self.r.fn_sends.at[offset], self.r.fn_receives.at[slot], {"fn": other}
        )

    def out_copy(self, offset, arriving=False):
        other = lax.rem(self.p + offset, self.n_pts)
        place = other if arriving else self.p
        src, dst = self.r.stage.at[self.mine(self.p)], self.total.at[self.mine(place)]
        return Reduction.remote(
            src, dst, self.r.sends.at[offset], self.r.receives.at[place], {"pts": other}
        )

    def local_copy(self):
        src, dst = self.r.stage.at[self.mine(self.p)], self.total.at[self.mine(self.p)]
        return pltpu.make_async_copy(src, dst, self.r.local_sem.at[0])

    def begin(self):
        for offset in range(1, self.n_fn):
            self.fn_copy(offset).start()
        self.r.slots[self.z] = self.r.stage[self.mine(self.p), :]

    def step(self):
        self.steps.pop(0)()

    def add(self):
        for offset in range(1, self.n_fn):
            self.fn_copy(offset, True).wait_recv()
        for offset in range(1, self.n_fn):
            self.fn_copy(offset).wait_send()
        sums = self.r.slots[0]
        for place in range(1, self.n_fn):
            sums = sums + self.r.slots[place]
        self.r.stage[self.mine(self.p), :] = sums
        self.local_copy().start()
        for offset in range(1, self.n_pts):
            self.out_copy(offset).start()

    def end(self):
        self.local_copy().wait()
        for offset in range(1, self.n_pts):
            self.out_copy(offset, True).wait_recv()
        for offset in range(1, self.n_pts):
            self.out_copy(offset).wait_send()


HALF = EXPERTS * D
PIECES = {
    ("out", 1, 1): ("out0", 512),
    ("in", 1, 1): ("in0", 512),
    ("out", 1, 0): ("out1", 768),
    ("in", 1, 0): ("in1", 512),
    ("out", 0, 1): ("out2", 512),
    ("in", 0, 1): ("in0", 768),
    ("out", 0, 0): ("out1", 768),
    ("in", 0, 0): ("in1", 512),
    "points": ("points", 256),
}
FIRST_ROW = {name: sum(rows for _, rows in list(PIECES.values())[:n]) for n, name in enumerate(PIECES)}
TOTAL_ROWS = sum(rows for _, rows in PIECES.values())


def function_rows(n_pts):
    return -(-(2 * D + 8) // (8 * n_pts)) * 8 * n_pts


WEIGHTS = ["ap", "ao", "ng", "nb", "ewi", "ebi", "ewo", "ebo", "gwi", "gbi", "gwo"]
IN_NAMES = ["x", "co", "ff", "counts", "present"] + WEIGHTS + ["cot"]
OUT_NAMES = ["q_out", "q_grad", "f_grad", "total", "f_total"]
KEPT_NAMES = ["kept_hi", "kept_lo", "kept_slope"]


def make_kernel(n_pts, n_fn, points, f_rows):
    tile = next(width for width in (256, 128) if points % width == 0)
    wide_tile = next(width for width in (512, 256, 128) if points % width == 0)
    f_tile = next(width for width in (512, 256, 128) if f_rows % width == 0)
    f_tiles = f_rows // f_tile
    inner = min(n_pts, GROUP)
    pts_stages = [("pts", 1, inner)]
    if n_pts > inner:
        pts_stages.append(("pts", inner, n_pts // inner))
    fn_stages = [("fn", 1, n_fn)]
    every = pts_stages + fn_stages
    syncs = {
        "P0": (fn_stages, 72),
        "P1": (fn_stages, 72),
        "S0": (every, 24),
        "S1": (every, 24),
        "dS1": (every, 24),
        "dC1": (every, 72),
        "dS0": (every, 24),
        "dC0": (every, 72),
    }
    scratch = dict(
        XS=pltpu.VMEM((6, D, points), f32),
        CUR=pltpu.VMEM((D, points), f32),
        COL=pltpu.VMEM((D, D), f32),
        TMP=pltpu.VMEM((32, D), f32),
        TMPK=pltpu.VMEM((16, 3 * D), f32),
        WC=pltpu.VMEM((LAYERS, 3 * D, D), bf16),
        WS=pltpu.VMEM((LAYERS, 3 * D, 3 * D), bf16),
        WF=pltpu.VMEM((LAYERS, 3 * D, 2 * D), bf16),
        WAO=pltpu.VMEM((LAYERS, 2, 3 * D, D), bf16),
        WI=pltpu.VMEM((4, 3 * D + 16, HID), bf16),
        WO=pltpu.VMEM((4, HID, 2 * D), bf16),
        BO=pltpu.VMEM((4, 32, D), bf16),
        BK=pltpu.VMEM((4, 16, 3 * D), bf16),
        GW=pltpu.VMEM((4, 32, D), bf16),
        GWK=pltpu.VMEM((4, 16, 3 * D), bf16),
        GWR=pltpu.VMEM((4, 32, D), bf16),
        CA=pltpu.VMEM((32, points), bf16),
        G=pltpu.VMEM((4, 8, points), f32),
        GB=pltpu.VMEM((4, 32, points), bf16),
        DL=pltpu.VMEM((4, 8, points), f32),
        GHH=pltpu.VMEM((3, HID, points), bf16),
        GHL=pltpu.VMEM((3, HID, points), bf16),
        GD=pltpu.VMEM((2, HID, points), f32),
        QCH=pltpu.VMEM((LAYERS, D, points), bf16),
        QCL=pltpu.VMEM((LAYERS, D, points), bf16),
        QSH=pltpu.VMEM((LAYERS, 3 * D, points), bf16),
        QSL=pltpu.VMEM((LAYERS, 3 * D, points), bf16),
        CR=pltpu.VMEM((LAYERS, 416, 3 * D), bf16),
        SE=pltpu.VMEM((LAYERS, 144, 3 * D), bf16),
        DK=pltpu.VMEM((432, D), bf16),
        PK=pltpu.VMEM((72, D), f32),
        ACC=pltpu.VMEM((416, D), f32),
        A4=pltpu.VMEM((4, 2 * D + 16, points), bf16),
        CC=pltpu.VMEM((4, 2 * D, points), bf16),
        OH=pltpu.VMEM((2, D, points), bf16),
        OL=pltpu.VMEM((2, D, points), bf16),
        DZH=pltpu.VMEM((4 * D, points), bf16),
        DZL=pltpu.VMEM((4 * D, points), bf16),
        LG=pltpu.VMEM((8, D, D), f32),
        GGA=pltpu.VMEM((4, 8, D), f32),
        GGB=pltpu.VMEM((4, 8, D), f32),
        dma_in=pltpu.SemaphoreType.DMA((10,)),
        dma_keep=pltpu.SemaphoreType.DMA((2, 2, 3)),
    )
    dma = pltpu.SemaphoreType.DMA
    for name, (stages, rows) in syncs.items():
        scratch[name] = [
            [pltpu.VMEM((stage[2], rows, D), f32), dma((stage[2],)), dma((stage[2],))] for stage in stages
        ]
    for buffers in dict.fromkeys(buffers for buffers, _ in PIECES.values()):
        rows = max(count for name, count in PIECES.values() if name == buffers)
        scratch[buffers] = Reduction.scratch(rows, n_pts, n_fn)
    scratch["functions"] = SharedReduction.scratch(function_rows(n_pts), n_pts, n_fn)
    shapes, tree = jax.tree.flatten(scratch)
    names = IN_NAMES + OUT_NAMES + KEPT_NAMES

    def kernel(*refs):
        r = SimpleNamespace(
            **dict(zip(names, refs)), **jax.tree.unflatten(tree, refs[len(names) :])
        )
        ex = {name: Exchange(stages, *zip(*vars(r)[name])) for name, (stages, _) in syncs.items()}
        piece = {
            name: Reduction(vars(r)[buffers], r.total, rows, FIRST_ROW[name], n_pts, n_fn)
            for name, (buffers, rows) in PIECES.items()
        }

        piece["functions"] = SharedReduction(r.functions, r.f_total, n_pts, n_fn)

        def staging(name):
            return piece[name].r.stage

        def small(layer):
            return staging("points").at[pl.ds(D + 32 * layer, 32)]

        barrier = pltpu.get_barrier_semaphore()
        greeted = 0
        for stage in every:
            for offset in range(1, stage[2]):
                _, device = Exchange.member(stage, offset)
                pl.semaphore_signal(barrier, inc=1, device_id=device, device_id_type=MESH)
                greeted += 1

        def weight_in(layer):
            into = r.GD.at[layer]
            every_copy = []
            for s in range(2):
                n = 4 * layer + 2 * s
                every_copy.append(
                    pltpu.make_async_copy(
                        r.ewi.at[layer, s],
                        into.at[pl.ds(s * EXPERTS * D, EXPERTS * D), pl.ds(0, FH)],
                        r.dma_in.at[n],
                    )
                )
                every_copy.append(
                    pltpu.make_async_copy(
                        r.ewo.at[layer, s],
                        into.at[:, pl.ds(FH + D * s, D)],
                        r.dma_in.at[n + 1],
                    )
                )
            return every_copy

        def points_in():
            return (
                pltpu.make_async_copy(r.x, r.q_grad, r.dma_in.at[8]),
                pltpu.make_async_copy(r.cot, r.q_out, r.dma_in.at[9]),
            )

        def kept(n, back):
            pairs = ((r.GHH, r.kept_hi), (r.GHL, r.kept_lo), (r.GD, r.kept_slope))
            copies = []
            for k, (near, far) in enumerate(pairs):
                ends = (near.at[n], far.at[n])
                src, dst = reversed(ends) if back else ends
                copies.append(pltpu.make_async_copy(src, dst, r.dma_keep.at[n, int(back), k]))
            return copies

        def start(copies):
            for copy in copies:
                copy.start()

        def wait(copies):
            for copy in copies:
                copy.wait()

        for copy in weight_in(0) + list(points_in()) + weight_in(1):
            copy.start()

        square, mask8 = head_masks()
        square = lambda: head_masks()[0]
        mask8 = lambda: head_masks()[1]

        def over_tiles(body, width=tile):
            def step(j, carry):
                body(pl.ds(pl.multiple_of(j * width, width), width))
                return carry

            lax.fori_loop(0, points // width, step, 0)

        def over(count, body):
            def step(j, carry):
                body(j)
                return carry

            lax.fori_loop(0, count, step, 0)

        def rows_of(e, width):
            return pl.ds(pl.multiple_of(e * width, width), width)

        def col(layer, j):
            return r.COL[:, layer * 5 + j : layer * 5 + j + 1]

        def bias_col(layer, j):
            return r.COL[:, 16 + layer * 5 + j : 17 + layer * 5 + j]

        norm_slot = {4: 0, 3: 0, 2: 1, 0: 2, 1: 3}

        def add_norm_grads(j, d_normed, unit):
            n = 2 * norm_slot[j]
            r.LG[n] += fold_lanes(d_normed * unit)
            r.LG[n + 1] += fold_lanes(d_normed)

        def clear_norm_grads(*which):
            for j in which:
                n = 2 * norm_slot[j]
                r.LG[n : n + 2] = jnp.zeros((2, D, D), f32)

        def put_norm_grads(layer, *which):
            for j in which:
                n = 2 * norm_slot[j]
                gain, bias = row_sum(r.LG[n]), row_sum(r.LG[n + 1])
                if j == 1 and layer == 0:
                    staging("functions")[2 * D : 2 * D + 1, :] = gain
                    staging("functions")[2 * D + 1 : 2 * D + 2, :] = bias
                    continue
                share = 1.0 / n_pts if j == 1 else 1.0
                small(layer)[j : j + 1, 0:D] = gain * share
                small(layer)[j : j + 1, D:] = bias * share

        def row_stack(ref, at, w):
            hi, lo = split(w)
            ref[at + (slice(0, D),)] = hi
            ref[at + (slice(D, 2 * D),)] = lo
            ref[at + (slice(2 * D, 3 * D),)] = hi

        def prepare_norms():
            r.COL[...] = jnp.zeros((D, D), f32)
            for layer in range(LAYERS):
                for j in range(5):
                    n = layer * 5 + j
                    r.COL[n : n + 1, :] = r.ng[j, layer : layer + 1]
                    r.COL[16 + n : 17 + n, :] = r.nb[j, layer : layer + 1]
            r.COL[...] = r.COL[...].T

        def prepare_func(layer):
            both = jnp.concatenate([r.ap[layer, 0, 1], r.ap[layer, 0, 2]], axis=1)
            row_stack(r.WF, (layer,), both)

        def prepare_attention(layer):
            row_stack(r.WC, (layer,), r.ap[layer, 0, 0])
            three = jnp.concatenate([r.ap[layer, 1, n] for n in range(3)], axis=1)
            row_stack(r.WS, (layer,), three)
            for c in range(2):
                row_stack(r.WAO, (layer, c), r.ao[layer, c])

        def small_rows(ref, n, hi, lo, count):
            tmp = r.TMP
            tmp[...] = jnp.zeros(tmp.shape, f32)
            tmp[0:count] = hi
            tmp[8 : 8 + count] = lo
            tmp[16 : 16 + count] = hi
            ref[n] = tmp[...].astype(bf16)

        def small_cols(ref, n, w):
            hi, lo = split(w)
            tmp = r.TMPK
            tmp[...] = jnp.zeros(tmp.shape, f32)
            tmp[0:4] = jnp.concatenate([hi.astype(f32), lo.astype(f32), hi.astype(f32)], axis=1)
            ref[n] = tmp[...].astype(bf16)

        def pair(v):
            hi, lo = split(v)
            return hi.astype(f32), lo.astype(f32)

        def prepare_experts(layer, s):
            n = 2 * layer + s
            staged = r.GD

            def body(e):
                w = staged[layer, rows_of(s * EXPERTS + e, D), 0:FH]
                hi, lo = split(w)
                cols = rows_of(e, FH)
                r.WI[n, 0:D, cols] = hi
                r.WI[n, D : 2 * D, cols] = lo
                r.WI[n, 2 * D : 3 * D, cols] = hi
                b_hi, b_lo = pair(r.ebi[layer, s, pl.ds(e, 1), :])
                r.WI[n, 3 * D : 3 * D + 16, cols] = jnp.concatenate(
                    [b_hi, b_lo, jnp.zeros((14, FH), f32)], axis=0
                ).astype(bf16)
                w = staged[layer, cols, FH + D * s : FH + D * (s + 1)]
                hi, lo = split(w)
                r.WO[n, cols, :] = jnp.concatenate([hi, lo], axis=1)

            over(EXPERTS, body)
            b_hi, b_lo = pair(r.ebo[layer, s])
            small_rows(r.BO, n, b_hi, b_lo, EXPERTS)
            small_cols(r.BK, n, r.ebo[layer, s])

        def prepare_gates(layer, s):
            n = 2 * layer + s
            for k in range(3):
                r.TMP[k : k + 1] = r.gwi[layer, k, s : s + 1]
            r.TMP[3:4] = r.gbi[layer, s : s + 1]
            hi, lo = pair(r.TMP[0:4])
            small_rows(r.GW, n, hi, lo, 4)
            hi, lo = pair(r.gwo[layer, s])
            small_rows(r.GWR, n, hi, lo, EXPERTS)
            small_cols(r.GWK, n, r.gwo[layer, s])

        def prepare_coords():
            hi, lo = pair(r.co[...])
            tmp = r.G
            tmp[...] = jnp.zeros(tmp.shape, f32)
            one = jnp.ones((1, points), f32)
            tmp[0, 0:3], tmp[0, 3:4] = hi, one
            tmp[1, 0:3], tmp[1, 3:4] = hi, one
            tmp[2, 0:3] = lo
            r.CA[...] = jnp.concatenate([tmp[n] for n in range(4)], axis=0).astype(bf16)

        def gates(n):
            def body(s):
                hidden, _ = gelu_both(tn(r.GW[n], r.CA[:, s]))
                logits = nn(r.GWK[n], k3(*split(hidden)))[0:8]
                real = lax.broadcasted_iota(jnp.int32, logits.shape, 0) < EXPERTS
                logits = jnp.where(real, logits, -1e30)
                power = jnp.exp(logits - jnp.max(logits, axis=0, keepdims=True))
                power = jnp.where(real, power, 0.0)
                share = power / jnp.sum(power, axis=0, keepdims=True)
                r.G[n, :, s] = share
                hi, lo = pair(share)
                r.GB[n, :, s] = jnp.concatenate([hi, hi, lo, jnp.zeros_like(hi)], axis=0).astype(bf16)

            over_tiles(body)

        def gates_back(n):
            r.GGA[n] = jnp.zeros((8, D), f32)
            r.GGB[n] = jnp.zeros((8, D), f32)

            def body(s):
                hidden, slope = gelu_both(tn(r.GW[n], r.CA[:, s]))
                hi, lo = pair(r.DL[n, :, s])
                stacked = jnp.concatenate([hi, hi, lo, jnp.zeros_like(hi)], axis=0).astype(bf16)
                h_hi, h_lo = split(hidden)
                first = nt(stacked, h_hi)
                r.GGA[n] += first[0:8] + first[16:24] + nt(stacked, h_lo)[0:8]
                d_hi, d_lo = split(tn(r.GWR[n], stacked) * slope)
                coords = r.CA[:, s]
                first = nt(coords, d_hi)
                r.GGB[n] += first[0:8] + first[16:24] + nt(coords, d_lo)[0:8]

            over_tiles(body)

        def func_parts(layer, f, s):
            unit, scale = normalise(r.ff[f, s, :].T)
            hi, lo = split(unit * col(layer, 1) + bias_col(layer, 1))
            kv = tn(r.WF[layer], k3(hi, lo))
            position = (
                lax.axis_index("fn") * f_rows
                + s.start
                + lax.broadcasted_iota(jnp.int32, (1, s.size), 1)
            )
            mask = jnp.where(position < r.counts[f], 1.0, 0.0).astype(f32)
            return unit, scale, hi, lo, head_softmax(kv[:D]) * mask, kv[D:]

        ones = lambda width: jnp.ones((16, width), bf16)

        def summary_part(k_hi, k_lo, v_hi, v_lo):
            width = k_hi.shape[1]
            v_ones = jnp.concatenate([v_hi, ones(width)], axis=0)
            wide = nt(v_ones, jnp.concatenate([k_hi, k_lo], axis=0))
            part = wide[:, :D] + wide[:, D:]
            return jnp.concatenate([part[:D] + nt(v_lo, k_hi), part[D:]], axis=0)

        def func_forward(layer):
            def per_function(f):
                r.ACC[0:144] = jnp.zeros((144, D), f32)

                def body(j):
                    _, _, _, _, keys, values = func_parts(layer, f, rows_of(j, f_tile))
                    r.ACC[0:144] += summary_part(*split(keys), *split(values))

                over(f_tiles, body)
                packed = pack_summary(r.ACC[0:D], r.ACC[D : D + 1], square())
                r.PK[rows_of(f, 24), :] = packed

            over(NF, per_function)
            return r.PK[...]

        def use_cross(layer, block):
            spread, rows = [], []
            for f in range(NF):
                wide, total = unpack_summary(block[24 * f : 24 * f + 24], square())
                spread.append(wide)
                rows.append(total * mask8())
            full = jnp.concatenate(spread + rows + [jnp.zeros((8, D), f32)], axis=0)
            hi, lo = split(full)
            r.CR[layer] = jnp.concatenate([hi, lo, hi], axis=1)

        def use_self(layer, block):
            wide, total = unpack_summary(block, square())
            full = jnp.concatenate([wide, total * mask8(), jnp.zeros((8, D), f32)], axis=0)
            hi, lo = split(full)
            r.SE[layer] = jnp.concatenate([hi, lo, hi], axis=1)

        def use_back(block):
            wide, total = unpack_summary(block, square())
            hi, lo = split(jnp.concatenate([wide, total, jnp.zeros((15, D), f32)], axis=0))
            r.DK[...] = jnp.concatenate([hi, lo, hi], axis=0)

        def keys_values_back(k_hi, k_lo, v_hi, v_lo):
            one = ones(k_hi.shape[1])
            zero = jnp.zeros_like(one)
            d_keys = tn(r.DK[...], jnp.concatenate([v_hi, one, v_hi, one, v_lo, zero], axis=0))
            both = nn(r.DK[0:272], k_hi)
            d_values = both[0:D] + both[144:272] + nn(r.DK[0:D], k_lo)
            return d_keys, d_values

        def func_backward(layer, into_keys, into_values, share):
            clear_norm_grads(1)
            into_keys[...] = jnp.zeros((D, D), f32)
            into_values[...] = jnp.zeros((D, D), f32)

            def per_function(f):
                use_back(r.PK[rows_of(f, 24), :])

                def body(j):
                    s = rows_of(j, f_tile)
                    unit, scale, a_hi, a_lo, keys, values = func_parts(layer, f, s)
                    d_keys, d_values = keys_values_back(*split(keys), *split(values))
                    d_z = jnp.concatenate([head_softmax_back(keys, d_keys), d_values], axis=0)
                    z_hi, z_lo = split(d_z)
                    wide = nt(jnp.concatenate([a_hi, a_lo], axis=0), z_hi)
                    full = wide[:D] + wide[D:] + nt(a_hi, z_lo)
                    into_keys[...] += full[:, :D] * share
                    into_values[...] += full[:, D:] * share
                    d_normed = nn_rows(r.WF, (layer,), z_hi, z_lo)
                    add_norm_grads(1, d_normed, unit)
                    d_rows = norm_back(d_normed, col(layer, 1), unit, scale).T
                    if layer == LAYERS - 1:
                        r.f_grad[f, s, :] = d_rows
                    else:
                        r.f_grad[f, s, :] += d_rows

                over(f_tiles, body)

            over(NF, per_function)
            put_norm_grads(layer, 1)

        def present_shares(width):
            total = r.present[0] + r.present[1] + r.present[2]
            total = jnp.full((1, width), total, jnp.int32).astype(f32)
            return [
                jnp.full((1, width), r.present[f], jnp.int32).astype(f32) / total for f in range(NF)
            ]

        def cross_apply(layer, q_hi, q_lo):
            applied = nn(r.CR[layer], k3(q_hi, q_lo))
            outs, inverse = [], []
            for f in range(NF):
                spread = head_spread(1.0 / applied[3 * D + 8 * f : 3 * D + 8 * f + 8])
                inverse.append(spread)
                outs.append(applied[D * f : D * (f + 1)] * spread)
            shares = present_shares(q_hi.shape[1])
            mixed = outs[0] * shares[0] + outs[1] * shares[1] + outs[2] * shares[2]
            return outs, inverse, shares, mixed

        def self_apply(layer, q_hi, q_lo):
            applied = nn(r.SE[layer], k3(q_hi, q_lo))
            spread = head_spread(1.0 / applied[D : D + 8])
            return applied[:D] * spread, spread

        def cross_forward(layer, x, s):
            unit, _ = normalise(x)
            normed = unit * col(layer, 0) + bias_col(layer, 0)
            q_hi, q_lo = split(head_softmax(tn(r.WC[layer], k3(*split(normed)))))
            r.QCH[layer, :, s] = q_hi
            r.QCL[layer, :, s] = q_lo
            _, _, _, mixed = cross_apply(layer, q_hi, q_lo)
            return x + tn(r.WAO[layer, 0], k3(*split(mixed)))

        def experts_forward(layer, which, x, s):
            n = 2 * layer + which
            j = 2 + 2 * which
            unit, _ = normalise(x)
            hi, lo = split(unit * col(layer, j) + bias_col(layer, j))
            stacked = jnp.concatenate([hi, hi, lo, ones(hi.shape[1])], axis=0)
            share = r.G[n, :, s]
            for c in range(HID // CHUNK):
                rows = slice(c * CHUNK, (c + 1) * CHUNK)
                e = c * CHUNK // FH
                value, slope = gelu_both(tn(r.WI[n, :, rows], stacked))
                h_hi, h_lo = split(value * share[e : e + 1])
                r.GHH[which, rows, s] = h_hi
                r.GHL[which, rows, s] = h_lo
                r.GD[which, rows, s] = slope * share[e : e + 1]
            both = tn(r.WO[n], r.GHH[which, :, s])
            more = tn(r.WO[n, :, 0:D], r.GHL[which, :, s])
            return x + tn(r.BO[n], r.GB[n, :, s]) + (both[:D] + both[D:] + more)

        def stream(layer, n):
            return 4 * layer + n - 1

        def first_stream(layer, s):
            return r.XS[stream(layer, 0), :, s] if layer else r.q_grad[s, :].T

        def phase_a(layer):
            r.ACC[0:144] = jnp.zeros((144, D), f32)

            xs = r.XS

            def cross(s):
                xs[stream(layer, 1), :, s] = cross_forward(layer, first_stream(layer, s), s)

            over_tiles(cross)

            def experts(s):
                x1 = xs[stream(layer, 1), :, s]
                xs[stream(layer, 2), :, s] = experts_forward(layer, 0, x1, s)

            over_tiles(experts, wide_tile)
            if layer == 0:
                start(kept(0, False))

            def sums(s):
                x2 = xs[stream(layer, 2), :, s]
                unit, _ = normalise(x2)
                normed = unit * col(layer, 3) + bias_col(layer, 3)
                qkv = tn(r.WS[layer], k3(*split(normed)))
                q_hi, q_lo = split(head_softmax(qkv[:D]))
                k_hi, k_lo = split(head_softmax(qkv[D : 2 * D]))
                v_hi, v_lo = split(qkv[2 * D :])
                r.QSH[layer, :, s] = jnp.concatenate([q_hi, k_hi, v_hi], axis=0)
                r.QSL[layer, :, s] = jnp.concatenate([q_lo, k_lo, v_lo], axis=0)
                r.ACC[0:144] += summary_part(k_hi, k_lo, v_hi, v_lo)

            over_tiles(sums)
            return pack_summary(r.ACC[0:D], r.ACC[D : D + 1], square())

        def self_forward(layer, s):
            mixed, _ = self_apply(layer, r.QSH[layer, 0:D, s], r.QSL[layer, 0:D, s])
            x2 = r.XS[stream(layer, 2), :, s]
            return x2 + tn(r.WAO[layer, 1], k3(*split(mixed)))

        def keep_cot(m, cot, s):
            c_hi, c_lo = split(cot)
            r.CC[m, 0:D, s] = c_hi
            r.CC[m, D : 2 * D, s] = c_lo

        def experts_backward(layer, which, x, cot, s):
            n = 2 * layer + which
            j = 2 + 2 * which
            c_hi, c_lo = r.CC[2 * which + 1, 0:D, s], r.CC[2 * which + 1, D : 2 * D, s]
            stacked = jnp.concatenate([c_hi, c_hi], axis=0)
            share = r.G[n, :, s]
            scores = share * nn(r.BK[n], k3(c_hi, c_lo))[0:8]
            place = lax.broadcasted_iota(jnp.int32, scores.shape, 0)

            part = None
            for c in range(HID // CHUNK):
                rows = slice(c * CHUNK, (c + 1) * CHUNK)
                back = nn(r.WO[n, rows, :], stacked) + nn(r.WO[n, rows, 0:D], c_lo)
                hidden = join(r.GHH[which, rows, s], r.GHL[which, rows, s])
                terms = (back * hidden).reshape(CHUNK // 8, 8, back.shape[1])
                terms = jnp.sum(terms, axis=0)
                part = terms if part is None else part + terms
                if (c + 1) * CHUNK % FH == 0:
                    total = jnp.sum(part, axis=0, keepdims=True)
                    scores = scores + jnp.where(place == c * CHUNK // FH, total, 0.0)
                    part = None
                z_hi, z_lo = split(back * r.GD[which, rows, s])
                r.GHH[2, rows, s] = z_hi
                r.GHL[2, rows, s] = z_lo
            both = nn(r.WI[n, 0 : 2 * D, :], r.GHH[2, :, s])
            d_normed = both[:D] + both[D:] + nn(r.WI[n, 0:D, :], r.GHL[2, :, s])
            r.DL[n, :, s] = scores - share * jnp.sum(scores, axis=0, keepdims=True)
            unit, scale = normalise(x)
            keep_normed(layer, j, unit, s, which * 2 + 1)
            add_norm_grads(j, d_normed, unit)
            return cot + norm_back(d_normed, col(layer, j), unit, scale)

        def keep_normed(layer, j, unit, s, n):
            hi, lo = split(unit * col(layer, j) + bias_col(layer, j))
            r.A4[n, 0:D, s] = lo
            r.A4[n, D : 2 * D, s] = hi

        def self_back_first(layer, d_x3, s):
            q_hi, q_lo = r.QSH[layer, 0:D, s], r.QSL[layer, 0:D, s]
            mixed, inverse = self_apply(layer, q_hi, q_lo)
            r.OH[1, :, s], r.OL[1, :, s] = split(mixed)
            c_hi, c_lo = split(d_x3)
            r.CC[2, 0:D, s] = c_hi
            r.CC[2, D : 2 * D, s] = c_lo
            d_num = nn_rows(r.WAO, (layer, 1), c_hi, c_lo) * inverse
            d_den = -head_rows(d_num * mixed)
            n_hi, n_lo = split(jnp.concatenate([d_num, d_den, jnp.zeros_like(d_den)], axis=0))
            r.ACC[0:144] += nt_pair(n_hi, n_lo, jnp.concatenate([q_hi, q_lo], axis=0), q_hi)
            both = tn(r.SE[layer, :, 0 : 2 * D], n_hi)
            d_q = both[:D] + both[D:] + tn(r.SE[layer, :, 0:D], n_lo)
            z_hi, z_lo = split(head_softmax_back(join(q_hi, q_lo), d_q))
            r.DZH[0:D, s] = z_hi
            r.DZL[0:D, s] = z_lo

        def phase_c(layer, tile_body):
            r.ACC[0:144] = jnp.zeros((144, D), f32)
            clear_norm_grads(4)

            def experts(s):
                r.CUR[:, s] = tile_body(s)

            over_tiles(experts, wide_tile)
            over_tiles(lambda s: self_back_first(layer, r.CUR[:, s], s))
            acc = r.ACC
            total = jnp.sum(acc[D : D + 8] * mask8(), axis=0, keepdims=True)
            return pack_summary(acc[0:D], total, square())

        def phase_d(layer, put, after_self, after_experts):
            r.ACC[...] = jnp.zeros(r.ACC.shape, f32)
            clear_norm_grads(3, 2, 0)
            n = 2 * layer

            def self_side(s):
                k_hi, k_lo = r.QSH[layer, D : 2 * D, s], r.QSL[layer, D : 2 * D, s]
                v_hi, v_lo = r.QSH[layer, 2 * D :, s], r.QSL[layer, 2 * D :, s]
                d_keys, d_values = keys_values_back(k_hi, k_lo, v_hi, v_lo)
                d_z = jnp.concatenate([head_softmax_back(join(k_hi, k_lo), d_keys), d_values], axis=0)
                z_hi, z_lo = split(d_z)
                r.DZH[D : 3 * D, s] = z_hi
                r.DZL[D : 3 * D, s] = z_lo
                d_normed = nn_rows(r.WS, (layer,), r.DZH[0 : 3 * D, s], r.DZL[0 : 3 * D, s])
                unit, scale = normalise(r.XS[stream(layer, 2), :, s])
                keep_normed(layer, 3, unit, s, 2)
                add_norm_grads(3, d_normed, unit)
                d_x2 = r.CUR[:, s] + norm_back(d_normed, col(layer, 3), unit, scale)
                r.CUR[:, s] = d_x2
                keep_cot(1, d_x2, s)

            over_tiles(self_side)
            spend(2.5)
            after_self()

            def experts(s):
                x1 = r.XS[stream(layer, 1), :, s]
                r.CUR[:, s] = experts_backward(layer, 0, x1, r.CUR[:, s], s)

            over_tiles(experts, wide_tile)
            spend(4)
            after_experts()

            def cross(s):
                d_x1 = r.CUR[:, s]
                q_hi, q_lo = r.QCH[layer, :, s], r.QCL[layer, :, s]
                outs, inverse, shares, mixed = cross_apply(layer, q_hi, q_lo)
                r.OH[0, :, s], r.OL[0, :, s] = split(mixed)
                c_hi, c_lo = split(d_x1)
                r.CC[0, 0:D, s] = c_hi
                r.CC[0, D : 2 * D, s] = c_lo
                d_o = nn_rows(r.WAO, (layer, 0), c_hi, c_lo)
                d_nums = [d_o * shares[f] * inverse[f] for f in range(NF)]
                d_dens = [-head_rows(d_nums[f] * outs[f]) for f in range(NF)]
                n_hi, n_lo = split(
                    jnp.concatenate(d_nums + d_dens + [jnp.zeros_like(d_dens[0])], axis=0)
                )
                r.ACC[...] += nt_pair(n_hi, n_lo, jnp.concatenate([q_hi, q_lo], axis=0), q_hi)
                both = tn(r.CR[layer, :, 0 : 2 * D], n_hi)
                d_q = both[:D] + both[D:] + tn(r.CR[layer, :, 0:D], n_lo)
                z_hi, z_lo = split(head_softmax_back(join(q_hi, q_lo), d_q))
                r.DZH[3 * D :, s] = z_hi
                r.DZL[3 * D :, s] = z_lo
                d_normed = nn_rows(r.WC, (layer,), z_hi, z_lo)
                unit, scale = normalise(first_stream(layer, s))
                keep_normed(layer, 0, unit, s, 0)
                add_norm_grads(0, d_normed, unit)
                put(s, d_x1 + norm_back(d_normed, col(layer, 0), unit, scale))

            over_tiles(cross)
            acc, blocks = r.ACC, []
            for f in range(NF):
                rows = acc[3 * D + 8 * f : 3 * D + 8 * f + 8] * mask8()
                total = jnp.sum(rows, axis=0, keepdims=True)
                blocks.append(pack_summary(acc[f * D : (f + 1) * D], total, square()))
            return jnp.concatenate(blocks, axis=0)

        def grad_in(layer, which):
            into = staging(("in", layer, which))
            m = 2 * which + 1

            def body(e):
                rows = rows_of(e, FH)
                wide = nt(r.A4[m], r.GHH[2, rows, :])
                more = nt(r.A4[m, D:, :], r.GHL[2, rows, :])
                into[rows_of(e, D), :] = wide[0:D] + wide[D : 2 * D] + more[0:D]
                bias = wide[2 * D : 2 * D + 1] + more[D : D + 1]
                small(layer)[pl.ds(8 + EXPERTS * which + e, 1), :] = bias

            over(EXPERTS, body)
            spend(2)

        def grad_out(layer, which):
            into = staging(("out", layer, which))
            m = 2 * which + 1

            def body(e):
                rows = rows_of(e, FH)
                h_hi, h_lo = r.GHH[which, rows, :], r.GHL[which, rows, :]
                down = pl.ds(pl.multiple_of(lax.rem(e, 2) * FH, FH), FH)
                across = pl.ds(pl.multiple_of(lax.div(e, 2) * D, D), D)
                into[down, across] = nt_pair(h_hi, h_lo, r.CC[m], r.CC[m, 0:D])

            over(EXPERTS, body)
            spend(1.6)

        def grad_gates(layer, which):
            n = 2 * layer + which
            wide = nt(r.GB[n], r.CC[2 * which + 1])
            bias = wide[0:4, :D] + wide[0:4, D:] + wide[16:20, :D]
            at = 16 + EXPERTS * which
            small(layer)[at : at + 4, 0:D] = bias
            gates_back(n)
            spend(1.6)
            small(layer)[at : at + 4, D:] = r.GGA[n, 0:4]
            at = 24 + 3 * which
            small(layer)[at : at + 3, 0:D] = r.GGB[n, 0:3]
            small(layer)[24 + which : 25 + which, D:] = r.GGB[n, 3:4]

        def grad_out_proj(c):
            m = 2 * c
            return nt_pair(r.OH[c], r.OL[c], r.CC[m], r.CC[m, 0:D])

        def grad_proj(c):
            rows = slice(0, 3 * D) if c else slice(3 * D, 4 * D)
            wide = nt(r.A4[2 * c, 0 : 2 * D, :], r.DZH[rows, :])
            return wide[:D] + wide[D:] + nt(r.A4[2 * c, D : 2 * D, :], r.DZL[rows, :])

        def grad_self(into, at):
            full = grad_proj(1)
            into[at : at + D, :] = full[:, 0 : 2 * D]
            into[at + D : at + 2 * D, 0:D] = full[:, 2 * D :]
            into[at + D : at + 2 * D, D:] = grad_out_proj(1)

        def grad_cross(into, at):
            into[at : at + D, 0:D] = grad_proj(0)
            into[at : at + D, D:] = grad_out_proj(0)

        running, clock = [], [0.0]

        def spend(us):
            clock[0] += us
            tick()

        def begin(name):
            piece[name].begin()
            running.append([piece[name], clock[0] + piece[name].waits[0]])

        def advance(entry):
            one = entry[0]
            one.step()
            if one.steps:
                entry[1] = clock[0] + one.waits[len(one.waits) - len(one.steps)]
            else:
                running.remove(entry)

        def tick():
            for entry in list(running):
                if entry[1] <= clock[0]:
                    advance(entry)

        def drain(name=None):
            while True:
                left = [entry for entry in running if name is None or entry[0] is piece[name]]
                if not left:
                    return
                entry = min(left, key=lambda each: each[1])
                clock[0] = max(clock[0], entry[1])
                advance(entry)

        prepare_norms()
        prepare_func(0)
        block = func_forward(0)
        pl.semaphore_wait(barrier, greeted)
        ex["P0"].start(0, block)
        prepare_func(1)
        for layer in range(LAYERS):
            prepare_attention(layer)
        prepare_coords()
        for m in (1, 3):
            r.A4[m, 2 * D :, :] = jnp.ones((16, points), bf16)
        for layer in range(LAYERS):
            for s in range(2):
                prepare_gates(layer, s)
        for copy in weight_in(0) + list(points_in()):
            copy.wait()
        for s in range(2):
            prepare_experts(0, s)
        gates(0)
        gates(1)
        ex["P1"].start(0, func_forward(1))
        use_cross(0, ex["P0"].finish(0))

        block = phase_a(0)
        ex["S0"].start(0, block)
        for copy in weight_in(1):
            copy.wait()
        for s in range(2):
            prepare_experts(1, s)
        gates(2)
        gates(3)
        use_cross(1, ex["P1"].finish(0))
        use_self(0, ex["S0"].finish_all())

        def first_self(s):
            r.XS[stream(0, 3), :, s] = self_forward(0, s)

        over_tiles(first_self)

        def first_out(s):
            x3 = r.XS[stream(0, 3), :, s]
            r.XS[stream(1, 0), :, s] = experts_forward(0, 1, x3, s)

        over_tiles(first_out, wide_tile)
        start(kept(1, False))
        wait(kept(0, False))
        block = phase_a(1)
        ex["S1"].start(0, block)
        use_self(1, ex["S1"].finish_all())

        wait(kept(1, False))

        def last_self(s):
            r.CUR[:, s] = self_forward(1, s)

        over_tiles(last_self)

        def turn(s):
            x3 = r.CUR[:, s]
            x4 = experts_forward(1, 1, x3, s)
            cot = r.q_out[s, :].T
            r.q_out[s, :] = x4.T
            keep_cot(3, cot, s)
            return experts_backward(1, 1, x3, cot, s)

        def put_current(s, v):
            r.CUR[:, s] = v
            keep_cot(3, v, s)

        def put_result(s, v):
            r.q_grad[s, :] = v.T

        for name in ("points", "functions"):
            staging(name)[...] = jnp.zeros(staging(name).shape, f32)
        block = phase_c(1, turn)
        ex["dS1"].start(0, block)
        put_norm_grads(1, 4)
        grad_out(1, 1)
        begin(("out", 1, 1))
        grad_in(1, 1)
        begin(("in", 1, 1))
        start(kept(1, True))
        ex["dS1"].start(1, ex["dS1"].finish(0))
        spend(1)
        grad_gates(1, 1)
        use_back(ex["dS1"].finish_all(1))
        spend(2)

        def after_self(layer):
            name = ("out", layer, 0)
            if not layer:
                drain(("out", 1, 0))
            grad_out(layer, 0)
            grad_self(staging(name), HALF)
            spend(0.8)
            begin(name)

        def after_experts(layer):
            if layer:
                start(kept(0, True))
            else:
                drain(("in", 1, 0))
            grad_in(layer, 0)
            begin(("in", layer, 0))

        block = phase_d(1, put_current, lambda: after_self(1), lambda: after_experts(1))
        ex["dC1"].start(0, block)
        spend(5)
        put_norm_grads(1, 3, 2, 0)
        wait(kept(1, True))
        grad_out(0, 1)
        begin(("out", 0, 1))
        grad_gates(1, 0)

        def second_experts(s):
            return experts_backward(0, 1, r.XS[stream(0, 3), :, s], r.CUR[:, s], s)

        ex["dC1"].start(1, ex["dC1"].finish(0))
        block = phase_c(0, second_experts)
        ex["dS0"].start(0, block)
        spend(6)
        put_norm_grads(0, 4)
        drain(("in", 1, 1))
        into = staging(("in", 0, 1))
        grad_cross(into, HALF)
        grad_in(0, 1)
        r.PK[...] = ex["dC1"].finish_all(1)
        ex["dS0"].start(1, ex["dS0"].finish(0))
        spend(1)
        keys, values = [into.at[pl.ds(HALF + D, D), pl.ds(n * D, D)] for n in range(2)]
        func_backward(1, keys, values, 1.0 / n_pts)
        begin(("in", 0, 1))
        spend(6)
        grad_gates(0, 1)
        use_back(ex["dS0"].finish_all(1))
        wait(kept(0, True))
        block = phase_d(0, put_result, lambda: after_self(0), lambda: after_experts(0))
        ex["dC0"].start(0, block)
        spend(5)
        put_norm_grads(0, 3, 2, 0)
        grad_cross(staging("points"), 0)
        grad_gates(0, 0)
        begin("points")
        ex["dC0"].start(1, ex["dC0"].finish(0))
        spend(2)
        r.PK[...] = ex["dC0"].finish_all(1)
        spend(3)
        keys, values = [staging("functions").at[pl.ds(n * D, D)] for n in range(2)]
        func_backward(0, keys, values, 1.0)
        begin("functions")
        spend(6)
        drain()

    return kernel, shapes


RESULTS = ["q_out", "q_grad", "f_grad"] + WEIGHTS
SMALL = ["ng", "nb", "ebi", "ebo", "gwi", "gbi", "gwo"]


def hand_out(*refs):
    sources = SimpleNamespace(**dict(zip(OUT_NAMES, refs)))
    refs = refs[len(OUT_NAMES) :]
    results = SimpleNamespace(**dict(zip(RESULTS, refs)))
    total, f_total, q_out, q_grad, f_grad, sems = refs[len(RESULTS) :]
    staged = [
        pltpu.make_async_copy(src, dst, sems.at[n])
        for n, (src, dst) in enumerate(
            [
                (sources.f_total, f_total),
                (sources.q_out, q_out),
                (sources.q_grad, q_grad),
                (sources.f_grad, f_grad),
            ]
            + [
                (sources.total.at[pl.ds(FIRST_ROW[name], count)], total.at[pl.ds(FIRST_ROW[name], count)])
                for name, (_, count) in PIECES.items()
            ]
        )
    ]
    for copy in staged:
        copy.start()

    def rows(name, start, count, lanes=slice(None)):
        lanes = pl.ds(lanes * D, D) if isinstance(lanes, int) else lanes
        return total.at[pl.ds(FIRST_ROW[name] + start, count), lanes]

    pairs = [(q_out, results.q_out), (q_grad, results.q_grad), (f_grad, results.f_grad)]
    for layer in range(LAYERS):
        for which in range(2):
            pairs.append((rows(("in", layer, which), 0, HALF), results.ewi.at[layer, which]))
            for n in range(2):
                into = results.ewo.at[layer, which, pl.ds(n * HALF, HALF)]
                pairs.append((rows(("out", layer, which), 0, HALF, n), into))
        self_rows, cross_rows = ("out", layer, 0), ("in", 0, 1)
        for n in range(3):
            pairs.append((rows(self_rows, HALF + n // 2 * D, D, n % 2), results.ap.at[layer, 1, n]))
        pairs.append((rows(self_rows, HALF + D, D, 1), results.ao.at[layer, 1]))
        if layer:
            for n, place in enumerate((0, 2, 3)):
                src = rows(cross_rows, HALF + place // 2 * D, D, place % 2)
                pairs.append((src, results.ap.at[layer, 0, n]))
            pairs.append((rows(cross_rows, HALF, D, 1), results.ao.at[layer, 0]))
        else:
            pairs.append((rows("points", 0, D, 0), results.ap.at[layer, 0, 0]))
            for n in range(2):
                pairs.append((f_total.at[pl.ds(n * D, D)], results.ap.at[layer, 0, 1 + n]))
            pairs.append((rows("points", 0, D, 1), results.ao.at[layer, 0]))
    for copy in staged:
        copy.wait()
    copies = [
        pltpu.make_async_copy(src, dst, sems.at[len(staged) + n]) for n, (src, dst) in enumerate(pairs)
    ]
    for copy in copies:
        copy.start()
    for layer in range(LAYERS):
        mine = rows("points", D + 32 * layer, 32)
        at = pl.ds(layer, 1)
        for j in range(5):
            if j == 1 and layer == 0:
                results.ng[j, at] = f_total[2 * D : 2 * D + 1]
                results.nb[j, at] = f_total[2 * D + 1 : 2 * D + 2]
            else:
                results.ng[j, at] = mine[j : j + 1, 0:D]
                results.nb[j, at] = mine[j : j + 1, D:]
        for which in range(2):
            at = EXPERTS * which
            results.ebi[layer, which] = mine[8 + at : 8 + at + EXPERTS, :]
            results.ebo[layer, which] = mine[16 + at : 16 + at + EXPERTS, 0:D]
            results.gwo[layer, which] = mine[16 + at : 16 + at + EXPERTS, D:]
            for k in range(3):
                row = 24 + 3 * which + k
                results.gwi[layer, k, which : which + 1] = mine[row : row + 1, 0:D]
            results.gbi[layer, which : which + 1] = mine[24 + which : 25 + which, D:]
    for copy in copies:
        copy.wait()


def solution(mesh):
    n_pts, n_fn = mesh.shape["pts"], mesh.shape["fn"]

    def per_device(*args):
        named = dict(zip(IN_NAMES, args))
        points, f_rows = named["x"].shape[0], named["ff"].shape[1]
        kernel, scratch = make_kernel(n_pts, n_fn, points, f_rows)
        named["ewi"] = named["ewi"].reshape(LAYERS, 2, EXPERTS * D, FH)
        named["ewo"] = named["ewo"].reshape(LAYERS, 2, HID, D)
        named["ng"], named["nb"] = [named[n].transpose(1, 0, 2) for n in ("ng", "nb")]
        named["gwi"] = named["gwi"].transpose(0, 2, 1, 3)
        vmem = pl.BlockSpec(memory_space=pltpu.VMEM)
        smem = pl.BlockSpec(memory_space=pltpu.SMEM)
        anywhere = pl.BlockSpec(memory_space=pl.ANY)
        places = {"counts": smem, "present": smem}
        for name in ["x", "cot", "ewi", "ewo", "total", "f_total"] + KEPT_NAMES:
            places[name] = anywhere
        like = lambda name: jax.ShapeDtypeStruct(named[name].shape, f32)
        out_shape = [like(n) for n in ("x", "x", "ff")]
        out_shape.append(jax.ShapeDtypeStruct((TOTAL_ROWS, 256), f32))
        out_shape.append(jax.ShapeDtypeStruct((function_rows(n_pts), D), f32))
        kept = (2, HID, points)
        out_shape += [jax.ShapeDtypeStruct(kept, kind) for kind in (bf16, bf16, f32)]
        outs = pl.pallas_call(
            kernel,
            out_shape=out_shape,
            in_specs=[places.get(n, vmem) for n in IN_NAMES],
            out_specs=[places.get(n, vmem) for n in OUT_NAMES + KEPT_NAMES],
            scratch_shapes=scratch,
            compiler_params=pltpu.CompilerParams(
                collective_id=0, has_side_effects=True, vmem_limit_bytes=int(63.5 * 2**20)
            ),
        )(*[named[n] for n in IN_NAMES])
        results = pl.pallas_call(
            hand_out,
            out_shape=out_shape[:3] + [like(n) for n in WEIGHTS],
            in_specs=[anywhere] * len(OUT_NAMES),
            out_specs=[vmem if n in SMALL else anywhere for n in RESULTS],
            scratch_shapes=[
                pltpu.VMEM(out_shape[n].shape, f32) for n in (3, 4, 0, 1, 2)
            ]
            + [pltpu.SemaphoreType.DMA((64,))],
            compiler_params=pltpu.CompilerParams(vmem_limit_bytes=60 * 2**20),
        )(*outs[: len(OUT_NAMES)])
        results = list(results)
        results[5], results[6] = results[5].transpose(1, 0, 2), results[6].transpose(1, 0, 2)
        results[11] = results[11].transpose(0, 2, 1, 3)
        results[7] = results[7].reshape(LAYERS, 2, EXPERTS, D, FH)
        results[9] = results[9].reshape(LAYERS, 2, EXPERTS, FH, D)
        return tuple(results)

    points = P(("pts", "fn"), None)
    return jax.shard_map(
        per_device,
        mesh=mesh,
        in_specs=(points, P(None, ("pts", "fn")), P(None, "fn", None)) + (P(),) * 13 + (points,),
        out_specs=(points, points, P(None, "fn", None)) + (P(),) * 11,
        check_vma=False,
    )
```

time: 960 us -> 188 us (0.20)
  matrix products: 341 us -> 0 us
  blocking collectives: 203 us -> 0 us
  waiting for transfers between devices: 195 us -> 0 us
  Pallas kernels: 0 us -> 187 us
  other arithmetic: 117 us -> 0 us
  local copies, waits for them, and re-layouts: 74.4 us -> 0 us
  between operations: 19.7 us -> 0.84 us
    dot_general x129 -> x0, matrix products: 341 us -> none  [the longest x12 103 us: expert_block(): jnp.einsum('erh,ehd->erd', hidden, w_out, precision=precise)]
    psum x6 -> x0, blocking collectives: 203 us -> none  [the longest x2 81.8 us: per_device(): self_sum, self_tot = lax.psum((self_part, self_part_tot), ('pts', 'fn'))]
    psum x3 -> x0, waiting for transfers between devices: 195 us -> none  [the longest x1 111 us: per_device(): lax.psum((stacked[0], stacked[1], stacked[2], stacked[3], stacked[4], sta...]
    pallas_call x0 -> x2, Pallas kernels: none -> 187 us  [the longest x1 179 us: per_device(): pl.pallas_call(kernel, out_shape=out_shape, in_specs=[places.get(n, vmem)...]
    reduce_sum x49 -> x0, other arithmetic: 51.8 us -> none  [the longest x15 22 us: layer_norm(): return centred * lax.rsqrt(variance + 1e-05) * gain_vec + bias_vec]
    unnamed x739 -> x0, local copies, waits for them, and re-layouts: 31.2 us -> none
    dot_general x28 -> x0, local copies, waits for them, and re-layouts: 28.6 us -> none  [the longest x4 8.26 us: expert_block(): jnp.einsum('rd,edh->erh', normed, w_in, precision=precise)]
    sub x8 -> x0, other arithmetic: 17.9 us -> none  [head_softmax(): return jax.nn.softmax(shaped, axis=-1)]
  transfers between devices with their start and end apart: 3 -> 0, of which waited for: 3 -> 0; matrix products, arithmetic and copies ran while one was open for 12% -> 0% of each run, Pallas kernels for 0% -> 0%
where the time goes in v1:
time: 188 us; the launch traced here: 187 us
  Pallas kernels  187 us (99%)
    pallas_call x1, Pallas kernels, per_device(): pl.pallas_call(kernel, out_shape=out_shape, in_specs=[places.get(n, vmem)...  179 us
    pallas_call x1, Pallas kernels, per_device(): pl.pallas_call(hand_out, out_shape=out_shape[:3] + [like(n) for n in WEIG...  7.11 us

profile of v1, /device:TPU:0, one launch (start us, length us, event | category | flops | bytes accessed | tf_op | source)
XLA Modules:
  0.0 187.4 jit_solution(17093400180273273040)
XLA Ops:
  0.7 179.5 %shard_map.272 = (f32[1024,128]{1,0:T(8,128)}, f32[1024,128]{1,0:T(8,128)}, f32[3,512,128]{2,1,0:T(8,128)}, f32[5120,256]{1,0:T(8,128)}, f32[320,128]{1,0:T(8,12...) custom-call(f32[1024,128]{1,0:T(8,128)} %refs_0_.1, ...), custom_call_target="tpu_custom_call" | custom-call | tf_op jit(solution)/shard_map/pallas_call | solution.py:1502
  180.1 7.1 %shard_map.273 = (f32[1024,128]{1,0:T(8,128)}, f32[1024,128]{1,0:T(8,128)}, f32[3,512,128]{2,1,0:T(8,128)}, f32[2,2,3,128,128]{4,3,2,1,0:T(8,128)}, f32[2,2,128,...) custom-call(f32[1024,128]{1,0:T(8,128)} %get-tuple-element.33.refs_0, ...), custom_call_target="tpu_custom_call" | custom-call | tf_op jit(solution)/shard_map/pallas_call | solution.py:1512
